TPU v7x, 32 devices: a whole 2x2x4 slice. The times are simulated.
32 devices in a mesh: dp: 8 (over y, x, core), ctx: 4 (over z).
Axes of the slice: x: 2, y: 2, z: 4, core: 2. Of those that a mesh axis runs over, the one named last changes fastest.
Arguments:
- queries: bfloat16 [4608, 2048], P(('dp', 'ctx')), parts along dimension 0, may hold values from -40 to 40
- keys: bfloat16 [4608, 2048], P(('dp', 'ctx')), parts along dimension 0, may hold values from -40 to 40
- values: bfloat16 [4608, 2048], P(('dp', 'ctx')), parts along dimension 0, may hold values from -6 to 6
- span_starts: int32 [8], P('dp'), parts along dimension 0, may hold values from 0 to 288, as said below
Outputs:
- attended: bfloat16 [4608, 2048], P(('dp', 'ctx')), parts along dimension 0
There are 8 independent parts, one for each index of `dp`. A program takes and returns all parts, laid end to end along the dimension named above; each array names one. Nothing has to cross between parts.
Inputs may be any that keep to these rules, and one draw needn't show every extreme that they name: `span_starts`: starts rise, and the 1 spans of 288 positions lie inside the document without intersecting.
All inputs are finite; a program needn't handle non-finite values.
Results may differ from a plain program's by a relative error of at most 0.0045.
Values may be sent and summed in bfloat16 or wider, within the bound.
A program may use at most 128 MiB of HBM per device.

v0:
```python
import jax
import jax.numpy as jnp
from jax import lax
from jax.sharding import PartitionSpec as P

HEADS = 16
HD = 128
SPAN = 288


def shifted(value, axis, steps):
    count = lax.axis_size(axis)
    pairs = [(source, (source + steps) % count) for source in range(count)]
    return lax.ppermute(value, axis, pairs)


def span_number(positions, span_starts):
    span_count = span_starts.shape[0]
    inside = (positions[:, None] >= span_starts[None, :]) & (
        positions[:, None] < span_starts[None, :] + SPAN
    )
    labels = jnp.arange(span_count, dtype=jnp.int32) + 1
    return jnp.sum(jnp.where(inside, labels[None, :], 0), axis=1)


def fold_block(operands):
    state_now, visible, group_query, key_heads, value_heads = operands
    row_max, row_sum, weighted = state_now
    scores = jnp.einsum(
        "qhd,khd->hqk", group_query, key_heads, preferred_element_type=jnp.float32
    ) * HD ** (-0.5)
    scores = jnp.where(visible[None], scores, -1e30)
    new_max = jnp.maximum(row_max, jnp.max(scores, axis=2))
    rescale = jnp.exp(row_max - new_max)
    weights = jnp.where(visible[None], jnp.exp(scores - new_max[:, :, None]), 0.0)
    new_sum = row_sum * rescale + jnp.sum(weights, axis=2)
    products = jnp.einsum(
        "hqk,khd->qhd",
        weights.astype(jnp.bfloat16),
        value_heads,
        preferred_element_type=jnp.float32,
    )
    new_weighted = weighted * rescale.T[:, :, None] + products
    return (new_max, new_sum, new_weighted)


def keep_block(operands):
    return operands[0]


def body(queries, keys, values, span_starts):
    tok_rows = queries.shape[0]
    row_width = queries.shape[1]
    loop_size = lax.axis_size("ctx")
    loop_index = lax.axis_index("ctx")
    local_rows = jnp.arange(tok_rows, dtype=jnp.int32)
    query_pos = loop_index * tok_rows + local_rows
    query_span = span_number(query_pos, span_starts)
    query_heads = queries.reshape(tok_rows, HEADS, HD)
    group_count = 2
    group_rows = tok_rows // group_count
    empty_state = tuple(
        (
            (
                jnp.full((HEADS, group_rows), -1e30, jnp.float32),
                jnp.zeros((HEADS, group_rows), jnp.float32),
                jnp.zeros((group_rows, HEADS, HD), jnp.float32),
            )
            for number in range(group_count)
        )
    )

    def absorb(running, block_pair, key_start):
        key_block, value_block = block_pair
        block_rows = key_block.shape[0]
        key_pos = key_start + jnp.arange(block_rows, dtype=jnp.int32)
        key_span = span_number(key_pos, span_starts)
        key_heads = key_block.reshape(block_rows, HEADS, HD)
        value_heads = value_block.reshape(block_rows, HEADS, HD)
        updated = []
        for group_index in range(group_count):
            row_start = group_index * group_rows
            group_pos = query_pos[row_start : row_start + group_rows]
            group_span = query_span[row_start : row_start + group_rows]
            group_query = query_heads[row_start : row_start + group_rows]
            visible = (key_pos[None, :] <= group_pos[:, None]) | (
                group_span[:, None] == key_span[None, :]
            ) & (group_span[:, None] > 0)
            operands = (running[group_index], visible, group_query, key_heads, value_heads)
            updated.append(lax.cond(jnp.any(visible), fold_block, keep_block, operands))
        return tuple(updated)

    stacked = jnp.stack([keys, values])
    own_state = absorb(empty_state, (keys, values), loop_index * tok_rows)

    def advance(step_index, loop_state):
        running, upward, downward = loop_state
        upward = shifted(upward, "ctx", 1)
        downward = shifted(downward, "ctx", -1)
        source_up = (loop_index - 1 - step_index) % loop_size
        source_down = (loop_index + 1 + step_index) % loop_size
        running = absorb(running, (upward[0], upward[1]), source_up * tok_rows)
        running = absorb(running, (downward[0], downward[1]), source_down * tok_rows)
        return (running, upward, downward)

    final_state, upward, downward = lax.fori_loop(
        0, (loop_size - 1) // 2, advance, (own_state, stacked, stacked)
    )
    upward = shifted(upward, "ctx", 1)
    source_last = (loop_index - loop_size // 2) % loop_size
    final_state = absorb(final_state, (upward[0], upward[1]), source_last * tok_rows)
    pieces = [weighted / row_sum.T[:, :, None] for row_max, row_sum, weighted in final_state]
    attended = jnp.concatenate(pieces, axis=0).reshape(tok_rows, row_width).astype(jnp.bfloat16)
    return attended


def solution(mesh):
    placed = (P(("dp", "ctx"), None), P(("dp", "ctx"), None), P(("dp", "ctx"), None), P("dp"))
    return jax.shard_map(
        body, mesh=mesh, in_specs=placed, out_specs=P(("dp", "ctx"), None), check_vma=False
    )
```

profile of v0, /device:TPU:16, one launch (start us, length us, event | category | flops | bytes accessed | tf_op | source)
XLA Modules:
  0.0 113.0 jit_solution(16896049705221562178)
XLA Ops:
  0.0 1.4 %pad_maximum_fusion = bf16[2,144,2048]{2,1,0:T(8,128)(2,1)S(1)} fusion(bf16[1,144,2048]{2,1,0:T(8,128)(2,1)} %bitcast.111, bf16[1,144,2048]{2,1,0:T(8,128)(2,1)} %bitcast.113), kind=kLoop, calls=%fused_computation.138 | loop fusion | flops 589824 | bytes 2359296 | tf_op jit(solution)/shard_map/stack | solution.py:93
  1.4 1.6 %collective-permute-start = (bf16[2,144,2048]{2,1,0:T(8,128)(2,1)S(1)}, bf16[2,144,2048]{2,1,0:T(8,128)(2,1)S(1)}, u32[]{:S(2)}, u32[]{:S(2)}) collective-permute-start(bf16[2,144,2048]{2,1,0:T(8,128)(2,1)S(1)} %pad_maximum_fusion), channel_id=1, source_target_pairs={{0,1},{1,2},{2,3},{3,0},{4,5},{5,6},{6,7},{7,4},{8,9},{9,10},{10,1... | collective-permute-start | bytes 3538952 | tf_op jit(solution)/shard_map/while/body/eval_jaxpr/ppermute | solution.py:14
  6.1 47.3 %collective-permute-done = bf16[2,144,2048]{2,1,0:T(8,128)(2,1)S(1)} collective-permute-done((bf16[2,144,2048]{2,1,0:T(8,128)(2,1)S(1)}, bf16[2,144,2048]{2,1,0:T(8,128)(2,1)S(1)}, u32[]{:S(2)}, u32[]{:S(2)}) %collective-permute-start) | collective-permute-done | bytes 1179680 | tf_op jit(solution)/shard_map/while/body/eval_jaxpr/ppermute | solution.py:14
  53.4 1.7 %collective-permute-start.2 = (bf16[2,144,2048]{2,1,0:T(8,128)(2,1)S(1)}, bf16[2,144,2048]{2,1,0:T(8,128)(2,1)}, u32[]{:S(2)}, u32[]{:S(2)}) collective-permute-start(bf16[2,144,2048]{2,1,0:T(8,128)(2,1)S(1)} %collective-permute-done), channel_id=1, source_target_pairs={{0,1},{1,2},{2,3},{3,0},{4,5},{5,6},{6,7},{7,4},{8,9},{9,10},{10,1... | collective-permute-start | bytes 3538952 | tf_op jit(solution)/shard_map/ppermute | solution.py:14
  55.7 2.4 %fusion.109 = (pred[]{:T(512)}, pred[72,144]{1,0:T(8,128)(4,1)}, pred[]{:T(512)}, pred[72,144]{1,0:T(8,128)(4,1)}, pred[]{:T(512)}, /*index=5*/pred[72,144]{1,0:...) fusion(pred[72]{0:T(512)(128)(4,1)} %get-tuple-element.418, ...), kind=kLoop, calls=%fused_computation.175 | loop fusion | flops 414712 | bytes 88856 | tf_op jit(solution)/shard_map/reduce_or | solution.py:90
  66.0 5.4 %conditional.12 = (f32[16,72]{1,0:T(8,128)}, f32[16,72]{1,0:T(8,128)S(1)}, f32[72,16,128]{2,0,1:T(8,128)S(1)}) conditional(s32[]{:T(128)} %convert_element_type.63, () %tuple.67, (pred[72,144]{1,0:T(8,128)(4,1)S(1)}, bf16[72,16,128]{2,1,0:T(8,128)(2,1)}, bf16[144,16,128]{2,1,0:T(8,128)(2,1)S(1)}, bf16[144,16,128]{2,1,0:T(8,128)(2,1)S(1)}) %tuple.196), branch_computations={%region_24.25_spmd, %region_25.28_spmd} | conditional | flops 86579712 | bytes 4136856 | solution.py:90
  66.0 1.6 %fusion.121 = (f32[16,72]{1,0:T(8,128)S(1)}, f32[16,72,144]{2,1,0:T(8,128)S(1)}) fusion(bf16[144,16,128]{2,1,0:T(8,128)(2,1)S(1)} %get-tuple-element.303, bf16[72,16,128]{2,1,0:T(8,128)(2,1)} %get-tuple-element.302, pred[72,144]{1,0:T(8,128)(4,1)S(1)} %get-tuple-element.207), kind=kOutput, calls=%fused_computation.187 | convolution fusion | flops 42963840 | bytes 1563264 | tf_op jit(solution)/shard_map/cond/branch_1_fun/qhd,khd->hqk/dot_general | solution.py:29
  69.4 1.2 %fusion.56 = f32[16,72]{1,0:T(8,128)S(1)} fusion(f32[16,72,144]{2,1,0:T(8,128)S(1)} %get-tuple-element.373, f32[16,72]{1,0:T(8,128)} %get-tuple-element.431, pred[72,144]{1,0:T(8,128)(4,1)S(1)} %get-tuple-element.207), kind=kLoop, calls=%fused_computation.75 | loop fusion | flops 496512 | bytes 683136 | tf_op jit(solution)/shard_map/cond/branch_1_fun/reduce_sum | solution.py:36
  71.3 5.6 %conditional.8 = (f32[16,72]{1,0:T(8,128)}, f32[16,72]{1,0:T(8,128)S(1)}, f32[72,16,128]{2,0,1:T(8,128)S(1)}) conditional(s32[]{:T(128)} %convert_element_type.59, () %tuple.61, (pred[72,144]{1,0:T(8,128)(4,1)}, bf16[72,16,128]{2,1,0:T(8,128)(2,1)}, bf16[144,16,128]{2,1,0:T(8,128)(2,1)}, bf16[144,16,128]{2,1,0:T(8,128)(2,1)}) %tuple.192), branch_computations={%region_4.5_spmd, %region_5.8_spmd} | conditional | flops 86579712 | bytes 6537680 | solution.py:90
  71.3 1.8 %fusion.120 = (f32[16,72]{1,0:T(8,128)S(1)}, f32[16,72,144]{2,1,0:T(8,128)S(1)}) fusion(bf16[144,16,128]{2,1,0:T(8,128)(2,1)} %get-tuple-element.278, bf16[72,16,128]{2,1,0:T(8,128)(2,1)} %get-tuple-element.277, pred[72,144]{1,0:T(8,128)(4,1)} %get-tuple-element.164), kind=kOutput, calls=%fused_computation.186 | convolution fusion | flops 42963840 | bytes 1563264 | tf_op jit(solution)/shard_map/cond/branch_1_fun/qhd,khd->hqk/dot_general | solution.py:29
  77.0 1.3 %slice_bitcast_fusion.2 = (bf16[18,8,16,128]{3,1,2,0:T(8,128)(2,1)S(1)}, bf16[18,8,16,128]{3,1,2,0:T(8,128)(2,1)S(1)}) fusion(bf16[2,144,2048]{2,1,0:T(8,128)(2,1)} %collective-permute-done.1), kind=kLoop, calls=%fused_computation.142 | loop fusion | bytes 2359296
  80.5 5.0 %conditional.13 = ((f32[16,72]{1,0:T(8,128)}, f32[16,72]{1,0:T(8,128)S(1)}, f32[72,16,128]{2,0,1:T(8,128)S(1)})) conditional(s32[]{:T(128)} %convert_element_type.62, (f32[16,72]{1,0:T(8,128)}, f32[16,72]{1,0:T(8,128)S(1)}, f32[72,16,128]{2,0,1:T(8,128)S(1)}) %conditional.12, (pred[72,144]{1,0:T(8,128)(4,1)}, bf16[72,16,128]{2,1,0:T(8,128)(2,1)}, ...), branch_computations={%region_28.29_spmd, %region_29.0_spmd} | conditional | flops 86726016 | bytes 4791228 | solution.py:90
  80.5 1.8 %fusion.117 = (f32[16,72]{1,0:T(8,128)S(1)}, f32[16,72,144]{2,1,0:T(8,128)S(1)}) fusion(bf16[144,16,128]{2,1,0:T(8,128)(2,1)} %get-tuple-element.307, bf16[72,16,128]{2,1,0:T(8,128)(2,1)} %get-tuple-element.306, pred[72,144]{1,0:T(8,128)(4,1)} %get-tuple-element.212), kind=kOutput, calls=%fused_computation.183 | convolution fusion | flops 42963840 | bytes 1563264 | tf_op jit(solution)/shard_map/while/body/eval_jaxpr/cond/branch_1_fun/qhd,khd->hqk/dot_general | solution.py:29
  85.5 5.0 %conditional.14 = ((f32[16,72]{1,0:T(8,128)}, f32[16,72]{1,0:T(8,128)S(1)}, f32[72,16,128]{2,0,1:T(8,128)S(1)})) conditional(s32[]{:T(128)} %convert_element_type.61, (f32[16,72]{1,0:T(8,128)}, f32[16,72]{1,0:T(8,128)S(1)}, f32[72,16,128]{2,0,1:T(8,128)S(1)}) %get-tuple-element.475, (pred[72,144]{1,0:T(8,128)(4,1)}, ...), branch_computations={%region_32.33_spmd, %region_33.0_spmd} | conditional | flops 86726016 | bytes 4791228 | solution.py:90
  85.5 1.8 %fusion.118 = (f32[16,72]{1,0:T(8,128)S(1)}, f32[16,72,144]{2,1,0:T(8,128)S(1)}) fusion(bf16[144,16,128]{2,1,0:T(8,128)(2,1)} %get-tuple-element.314, bf16[72,16,128]{2,1,0:T(8,128)(2,1)} %get-tuple-element.313, pred[72,144]{1,0:T(8,128)(4,1)} %get-tuple-element.219), kind=kOutput, calls=%fused_computation.184 | convolution fusion | flops 42963840 | bytes 1563264 | tf_op jit(solution)/shard_map/while/body/eval_jaxpr/cond/branch_1_fun/qhd,khd->hqk/dot_general | solution.py:29
  90.5 5.0 %conditional.9 = ((f32[16,72]{1,0:T(8,128)}, f32[16,72]{1,0:T(8,128)S(1)}, f32[72,16,128]{2,0,1:T(8,128)S(1)})) conditional(s32[]{:T(128)} %convert_element_type.58, (f32[16,72]{1,0:T(8,128)}, f32[16,72]{1,0:T(8,128)S(1)}, f32[72,16,128]{2,0,1:T(8,128)S(1)}) %conditional.8, (pred[72,144]{1,0:T(8,128)(4,1)}, bf16[72,16,128]{2,1,0:T(8,128)(2,1)}, ...), branch_computations={%region_8.9_spmd, %region_9.12_spmd} | conditional | flops 86726016 | bytes 4791228 | solution.py:90
  90.5 1.8 %fusion.114 = (f32[16,72]{1,0:T(8,128)S(1)}, f32[16,72,144]{2,1,0:T(8,128)S(1)}) fusion(bf16[144,16,128]{2,1,0:T(8,128)(2,1)} %get-tuple-element.282, bf16[72,16,128]{2,1,0:T(8,128)(2,1)} %get-tuple-element.281, pred[72,144]{1,0:T(8,128)(4,1)} %get-tuple-element.178), kind=kOutput, calls=%fused_computation.180 | convolution fusion | flops 42963840 | bytes 1563264 | tf_op jit(solution)/shard_map/while/body/eval_jaxpr/cond/branch_1_fun/qhd,khd->hqk/dot_general | solution.py:29
  95.5 5.0 %conditional.10 = ((f32[16,72]{1,0:T(8,128)}, f32[16,72]{1,0:T(8,128)S(1)}, f32[72,16,128]{2,0,1:T(8,128)S(1)})) conditional(s32[]{:T(128)} %convert_element_type.57, (f32[16,72]{1,0:T(8,128)}, f32[16,72]{1,0:T(8,128)S(1)}, f32[72,16,128]{2,0,1:T(8,128)S(1)}) %get-tuple-element.472, (pred[72,144]{1,0:T(8,128)(4,1)}, ...), branch_computations={%region_12.13_spmd, %region_13.16_spmd} | conditional | flops 86726016 | bytes 4791228 | solution.py:90
  95.5 1.8 %fusion.115 = (f32[16,72]{1,0:T(8,128)S(1)}, f32[16,72,144]{2,1,0:T(8,128)S(1)}) fusion(bf16[144,16,128]{2,1,0:T(8,128)(2,1)} %get-tuple-element.289, bf16[72,16,128]{2,1,0:T(8,128)(2,1)} %get-tuple-element.288, pred[72,144]{1,0:T(8,128)(4,1)} %get-tuple-element.192), kind=kOutput, calls=%fused_computation.181 | convolution fusion | flops 42963840 | bytes 1563264 | tf_op jit(solution)/shard_map/while/body/eval_jaxpr/cond/branch_1_fun/qhd,khd->hqk/dot_general | solution.py:29
  100.5 1.4 %slice_bitcast_fusion = (bf16[18,8,16,128]{3,1,2,0:T(8,128)(2,1)S(1)}, bf16[18,8,16,128]{3,1,2,0:T(8,128)(2,1)S(1)}) fusion(bf16[2,144,2048]{2,1,0:T(8,128)(2,1)} %collective-permute-done.2), kind=kLoop, calls=%fused_computation.140 | loop fusion | bytes 2359296
  102.9 4.4 %conditional.15 = ((f32[16,72]{1,0:T(8,128)S(1)}, f32[72,16,128]{2,0,1:T(8,128)S(1)})) conditional(s32[]{:T(128)} %convert_element_type.60, (f32[16,72]{1,0:T(8,128)S(1)}, f32[72,16,128]{2,0,1:T(8,128)S(1)}) %tuple.71, (pred[72,144]{1,0:T(8,128)(4,1)}, bf16[72,16,128]{2,1,0:T(8,128)(2,1)}, bf16[144,16,128]{2,1,0:T(8,128)(2,1)}, ...), branch_computations={%region_36.37_spmd, %region_37.40_spmd} | conditional | flops 86726016 | bytes 4782004 | solution.py:90
  102.9 1.8 %fusion.119 = (f32[16,72]{1,0:T(8,128)S(1)}, f32[16,72,144]{2,1,0:T(8,128)S(1)}) fusion(bf16[144,16,128]{2,1,0:T(8,128)(2,1)} %get-tuple-element.321, bf16[72,16,128]{2,1,0:T(8,128)(2,1)} %get-tuple-element.320, pred[72,144]{1,0:T(8,128)(4,1)} %get-tuple-element.227), kind=kOutput, calls=%fused_computation.185 | convolution fusion | flops 42963840 | bytes 1563264 | tf_op jit(solution)/shard_map/cond/branch_1_fun/qhd,khd->hqk/dot_general | solution.py:29
  107.6 4.3 %conditional.11 = ((f32[16,72]{1,0:T(8,128)S(1)}, f32[72,16,128]{2,0,1:T(8,128)S(1)})) conditional(s32[]{:T(128)} %convert_element_type.56, (f32[16,72]{1,0:T(8,128)S(1)}, f32[72,16,128]{2,0,1:T(8,128)S(1)}) %tuple.65, (pred[72,144]{1,0:T(8,128)(4,1)}, bf16[72,16,128]{2,1,0:T(8,128)(2,1)S(1)}, bf16[144,16,128]{2,1,0:T(8,128)(2,1)}, ...), branch_computations={%region_16.17_spmd, %region_17.0_spmd} | conditional | flops 86726016 | bytes 4782004 | solution.py:90
  107.6 1.7 %fusion.116 = (f32[16,72]{1,0:T(8,128)S(1)}, f32[16,72,144]{2,1,0:T(8,128)S(1)}) fusion(bf16[144,16,128]{2,1,0:T(8,128)(2,1)} %get-tuple-element.296, bf16[72,16,128]{2,1,0:T(8,128)(2,1)S(1)} %get-tuple-element.295, pred[72,144]{1,0:T(8,128)(4,1)} %get-tuple-element.202), kind=kOutput, calls=%fused_computation.182 | convolution fusion | flops 42963840 | bytes 1563264 | tf_op jit(solution)/shard_map/cond/branch_1_fun/qhd,khd->hqk/dot_general | solution.py:29
  (91 shorter events, 34.6 us)
Async XLA Ops:
  0.0 63.1 %copy-start = (bf16[144,2048]{1,0:T(8,128)(2,1)S(1)}, bf16[144,2048]{1,0:T(8,128)(2,1)}, u32[]{:S(2)}) copy-start(bf16[144,2048]{1,0:T(8,128)(2,1)} %param.22) | copy-start | bytes 1769476
  1.4 61.9 %copy-start.1 = (bf16[144,2048]{1,0:T(8,128)(2,1)S(1)}, bf16[144,2048]{1,0:T(8,128)(2,1)}, u32[]{:S(2)}) copy-start(bf16[144,2048]{1,0:T(8,128)(2,1)} %param.21) | copy-start | bytes 1769476
  1.4 51.9 %collective-permute-start = (bf16[2,144,2048]{2,1,0:T(8,128)(2,1)S(1)}, bf16[2,144,2048]{2,1,0:T(8,128)(2,1)S(1)}, u32[]{:S(2)}, u32[]{:S(2)}) collective-permute-start(bf16[2,144,2048]{2,1,0:T(8,128)(2,1)S(1)} %pad_maximum_fusion), channel_id=1, source_target_pairs={{0,1},{1,2},{2,3},{3,0},{4,5},{5,6},{6,7},{7,4},{8,9},{9,10},{10,1... | collective-permute-start | bytes 3538952 | tf_op jit(solution)/shard_map/while/body/eval_jaxpr/ppermute | solution.py:14
  3.1 73.9 %collective-permute-start.1 = (bf16[2,144,2048]{2,1,0:T(8,128)(2,1)S(1)}, bf16[2,144,2048]{2,1,0:T(8,128)(2,1)}, u32[]{:S(2)}, u32[]{:S(2)}) collective-permute-start(bf16[2,144,2048]{2,1,0:T(8,128)(2,1)S(1)} %pad_maximum_fusion), channel_id=1, source_target_pairs={{0,3},{1,0},{2,1},{3,2},{4,7},{5,4},{6,5},{7,6},{8,11},{9,8},{10,9... | collective-permute-start | bytes 3538952 | tf_op jit(solution)/shard_map/while/body/eval_jaxpr/ppermute | solution.py:14
  53.4 47.1 %collective-permute-start.2 = (bf16[2,144,2048]{2,1,0:T(8,128)(2,1)S(1)}, bf16[2,144,2048]{2,1,0:T(8,128)(2,1)}, u32[]{:S(2)}, u32[]{:S(2)}) collective-permute-start(bf16[2,144,2048]{2,1,0:T(8,128)(2,1)S(1)} %collective-permute-done), channel_id=1, source_target_pairs={{0,1},{1,2},{2,3},{3,0},{4,5},{5,6},{6,7},{7,4},{8,9},{9,10},{10,1... | collective-permute-start | bytes 3538952 | tf_op jit(solution)/shard_map/ppermute | solution.py:14
  63.1 1.1 %copy-start.2 = (bf16[144,2048]{1,0:T(8,128)(2,1)S(1)}, bf16[144,2048]{1,0:T(8,128)(2,1)}, u32[]{:S(2)}) copy-start(bf16[144,2048]{1,0:T(8,128)(2,1)} %param.20) | copy-start | bytes 1769476
  63.3 2.7 %copy-start.3 = (bf16[18,8,16,128]{3,2,1,0:T(8,128)(2,1)}, bf16[18,8,16,128]{3,2,1,0:T(8,128)(2,1)S(1)}, u32[]{:S(2)}) copy-start(bf16[18,8,16,128]{3,2,1,0:T(8,128)(2,1)S(1)} %copy.34) | copy-start | bytes 1769476
  64.3 1.7 %copy-start.5 = (bf16[18,8,16,128]{3,2,1,0:T(8,128)(2,1)}, bf16[18,8,16,128]{3,2,1,0:T(8,128)(2,1)S(1)}, u32[]{:S(2)}) copy-start(bf16[18,8,16,128]{3,2,1,0:T(8,128)(2,1)S(1)} %copy.33) | copy-start | bytes 1769476
  64.3 1.7 %copy-start.14 = (pred[72,144]{1,0:T(8,128)(4,1)S(1)}, pred[72,144]{1,0:T(8,128)(4,1)}, u32[]{:S(2)}) copy-start(pred[72,144]{1,0:T(8,128)(4,1)} %get-tuple-element.407) | copy-start | bytes 31108
  71.3 2.4 %copy-start.4 = (bf16[144,16,128]{2,1,0:T(8,128)(2,1)S(1)}, bf16[144,16,128]{2,1,0:T(8,128)(2,1)}, u32[]{:S(2)}) copy-start(bf16[144,16,128]{2,1,0:T(8,128)(2,1)} %get-tuple-element.279) | copy-start | bytes 1769476 | tf_op jit(solution)/shard_map/cond
  71.3 2.4 %copy-start.13 = (pred[72,144]{1,0:T(8,128)(4,1)S(1)}, pred[72,144]{1,0:T(8,128)(4,1)}, u32[]{:S(2)}) copy-start(pred[72,144]{1,0:T(8,128)(4,1)} %get-tuple-element.164) | copy-start | bytes 31108 | tf_op jit(solution)/shard_map/cond
  80.5 2.5 %copy-start.12 = (pred[72,144]{1,0:T(8,128)(4,1)S(1)}, pred[72,144]{1,0:T(8,128)(4,1)}, u32[]{:S(2)}) copy-start(pred[72,144]{1,0:T(8,128)(4,1)} %get-tuple-element.212) | copy-start | bytes 31108 | tf_op jit(solution)/shard_map/while/body/eval_jaxpr/cond
  85.5 2.5 %copy-start.11 = (pred[72,144]{1,0:T(8,128)(4,1)S(1)}, pred[72,144]{1,0:T(8,128)(4,1)}, u32[]{:S(2)}) copy-start(pred[72,144]{1,0:T(8,128)(4,1)} %get-tuple-element.219) | copy-start | bytes 31108 | tf_op jit(solution)/shard_map/while/body/eval_jaxpr/cond
  90.5 2.5 %copy-start.10 = (pred[72,144]{1,0:T(8,128)(4,1)S(1)}, pred[72,144]{1,0:T(8,128)(4,1)}, u32[]{:S(2)}) copy-start(pred[72,144]{1,0:T(8,128)(4,1)} %get-tuple-element.178) | copy-start | bytes 31108 | tf_op jit(solution)/shard_map/while/body/eval_jaxpr/cond
  95.5 2.5 %copy-start.9 = (pred[72,144]{1,0:T(8,128)(4,1)S(1)}, pred[72,144]{1,0:T(8,128)(4,1)}, u32[]{:S(2)}) copy-start(pred[72,144]{1,0:T(8,128)(4,1)} %get-tuple-element.192) | copy-start | bytes 31108 | tf_op jit(solution)/shard_map/while/body/eval_jaxpr/cond
  102.9 4.7 %copy-start.6 = (bf16[9,8,16,128]{3,2,1,0:T(8,128)(2,1)S(1)}, bf16[9,8,16,128]{3,2,1,0:T(8,128)(2,1)}, u32[]{:S(2)}) copy-start(bf16[9,8,16,128]{3,2,1,0:T(8,128)(2,1)} %copy.32) | copy-start | bytes 884740
  102.9 2.5 %copy-start.8 = (pred[72,144]{1,0:T(8,128)(4,1)S(1)}, pred[72,144]{1,0:T(8,128)(4,1)}, u32[]{:S(2)}) copy-start(pred[72,144]{1,0:T(8,128)(4,1)} %get-tuple-element.227) | copy-start | bytes 31108 | tf_op jit(solution)/shard_map/cond
  107.6 2.4 %copy-start.7 = (pred[72,144]{1,0:T(8,128)(4,1)S(1)}, pred[72,144]{1,0:T(8,128)(4,1)}, u32[]{:S(2)}) copy-start(pred[72,144]{1,0:T(8,128)(4,1)} %get-tuple-element.202) | copy-start | bytes 31108 | tf_op jit(solution)/shard_map/cond
where the time goes:
time: 114 us; the launch traced here: 113 us
  waiting for transfers between devices  47.3 us (41%)
  other arithmetic  23.3 us (20%)
  matrix products  20.2 us (18%)
  local copies, waits for them, and re-layouts  12.5 us (11%)
  between operations  5.86 us (5%)
  starting transfers between devices  3.79 us (3%)
    ppermute x3, waiting for transfers between devices, shifted(): return lax.ppermute(value, axis, pairs)  47.3 us
    dot_general x8, matrix products, fold_block(): jnp.einsum('qhd,khd->hqk', group_query, key_heads, preferred_element_type...  14 us
    unnamed x28, local copies, waits for them, and re-layouts  8.74 us
    dot_general x8, matrix products, fold_block(): jnp.einsum('hqk,khd->qhd', weights.astype(jnp.bfloat16), value_heads, pre...  6.17 us
    reduce_sum x8, other arithmetic, fold_block(): new_sum = row_sum * rescale + jnp.sum(weights, axis=2)  5.83 us
    add x8, other arithmetic, fold_block(): new_sum = row_sum * rescale + jnp.sum(weights, axis=2)  5.65 us
    transpose x6, other arithmetic, fold_block(): new_weighted = weighted * rescale.T[:, :, None] + products  4.23 us
    ppermute x3, starting transfers between devices, shifted(): return lax.ppermute(value, axis, pairs)  3.79 us
  transfers between devices with their start and end apart: 3, of which 1 were waited for; matrix products, arithmetic and copies ran while one was open for 36% of the time, Pallas kernels for 0%

commit v1 on v0

--- a/solution.py
+++ b/solution.py
@@ -1,6 +1,11 @@
+import functools
+import math
+
 import jax
 import jax.numpy as jnp
 from jax import lax
+from jax.experimental import pallas as pl
+from jax.experimental.pallas import tpu as pltpu
 from jax.sharding import PartitionSpec as P
 
 HEADS = 16
@@ -48,7 +53,7 @@
     return operands[0]
 
 
-def body(queries, keys, values, span_starts):
+def ring_body(queries, keys, values, span_starts):
     tok_rows = queries.shape[0]
     row_width = queries.shape[1]
     loop_size = lax.axis_size("ctx")
@@ -114,7 +119,177 @@
     return attended
 
 
+def exchange_kernel(
+    count, images, starts_ref, q_ref, k_ref, v_ref, out_ref,
+    q_all, k_all, v_all, o_all, bias,
+    in_send, in_recv, in_local, out_send, out_recv, out_local,
+):
+    me = lax.axis_index("ctx")
+    rows = q_ref.shape[0]
+    length = rows * count
+    own_heads = HEADS // count
+    half = count // 2
+    side = me // half
+    far = [(1 - side) * half + (me + i) % half for i in range(half)]
+    near = [side * half + (me + i) % half for i in range(1, half)]
+    peers = far + near
+    my_rows = pl.ds(pl.multiple_of(me * rows, rows), rows)
+    sources = (q_ref, k_ref, v_ref)
+    landing = (q_all, k_all, v_all)
+
+    def columns(owner, head):
+        return pl.ds(pl.multiple_of((owner * own_heads + head) * HD, HD), HD)
+
+    def rows_of(device):
+        return pl.ds(pl.multiple_of(device * rows, rows), rows)
+
+    def operand_copy(which, head, peer):
+        return pltpu.make_async_remote_copy(
+            src_ref=sources[which].at[:, columns(peer, head)],
+            dst_ref=landing[which].at[head, my_rows, :],
+            send_sem=in_send.at[which, head, peer],
+            recv_sem=in_recv.at[which, head, me],
+            device_id={"ctx": peer},
+            device_id_type=pl.DeviceIdType.MESH,
+        )
+
+    def operand_arrival(which, head, peer):
+        return pltpu.make_async_remote_copy(
+            src_ref=sources[which].at[:, columns(peer, head)],
+            dst_ref=landing[which].at[head, rows_of(peer), :],
+            send_sem=in_send.at[which, head, peer],
+            recv_sem=in_recv.at[which, head, peer],
+            device_id={"ctx": peer},
+            device_id_type=pl.DeviceIdType.MESH,
+        )
+
+    def operand_local(which, head):
+        return pltpu.make_async_copy(
+            sources[which].at[:, columns(me, head)],
+            landing[which].at[head, my_rows, :],
+            in_local.at[which, head],
+        )
+
+    def result_copy(head, peer):
+        return pltpu.make_async_remote_copy(
+            src_ref=o_all.at[head, rows_of(peer), :],
+            dst_ref=out_ref.at[:, columns(me, head)],
+            send_sem=out_send.at[head, peer],
+            recv_sem=out_recv.at[head, me],
+            device_id={"ctx": peer},
+            device_id_type=pl.DeviceIdType.MESH,
+        )
+
+    def result_arrival(head, peer):
+        return pltpu.make_async_remote_copy(
+            src_ref=o_all.at[head, rows_of(peer), :],
+            dst_ref=out_ref.at[:, columns(peer, head)],
+            send_sem=out_send.at[head, peer],
+            recv_sem=out_recv.at[head, peer],
+            device_id={"ctx": peer},
+            device_id_type=pl.DeviceIdType.MESH,
+        )
+
+    def result_local(head):
+        return pltpu.make_async_copy(
+            o_all.at[head, my_rows, :], out_ref.at[:, columns(me, head)], out_local.at[head]
+        )
+
+    barrier = pltpu.get_barrier_semaphore()
+    for peer in peers:
+        pl.semaphore_signal(
+            barrier, inc=1, device_id={"ctx": peer}, device_id_type=pl.DeviceIdType.MESH
+        )
+    pl.semaphore_wait(barrier, count - 1)
+
+    def send_head(head, carry):
+        for peer in peers:
+            for which in range(3):
+                operand_copy(which, head, peer).start()
+        for which in range(3):
+            operand_local(which, head).start()
+        return carry
+
+    lax.fori_loop(0, own_heads, send_head, 0)
+
+    query_pos = lax.broadcasted_iota(jnp.int32, (length, length), 0)
+    key_pos = lax.broadcasted_iota(jnp.int32, (length, length), 1)
+    visible = key_pos <= query_pos
+    for image in range(images):
+        first = starts_ref[image]
+        inside = (
+            (query_pos >= first) & (query_pos < first + SPAN)
+            & (key_pos >= first) & (key_pos < first + SPAN)
+        )
+        visible = visible | inside
+    bias[...] = jnp.where(visible, 0.0, -1e30)
+
+    def attend_head(head, carry):
+        for which in range(3):
+            operand_local(which, head).wait()
+            for peer in peers:
+                operand_arrival(which, head, peer).wait_recv()
+        scores = lax.dot_general(
+            q_all[head], k_all[head], (((1,), (1,)), ((), ())),
+            preferred_element_type=jnp.float32,
+        ) * (HD ** (-0.5) * math.log2(math.e))
+        scores = scores + bias[...]
+        weights = jnp.exp2(scores - jnp.max(scores, axis=1, keepdims=True))
+        total = jnp.sum(weights, axis=1, keepdims=True)
+        mixed = jnp.dot(
+            weights.astype(jnp.bfloat16), v_all[head], preferred_element_type=jnp.float32
+        )
+        o_all[head] = (mixed / total).astype(jnp.bfloat16)
+        for peer in peers:
+            result_copy(head, peer).start()
+        result_local(head).start()
+        return carry
+
+    lax.fori_loop(0, own_heads, attend_head, 0)
+
+    def finish_head(head, carry):
+        result_local(head).wait()
+        for peer in peers:
+            for which in range(3):
+                operand_copy(which, head, peer).wait_send()
+            result_copy(head, peer).wait_send()
+            result_arrival(head, peer).wait_recv()
+        return carry
+
+    lax.fori_loop(0, own_heads, finish_head, 0)
+
+
+def exchange_body(count, queries, keys, values, span_starts):
+    rows = queries.shape[0]
+    length = rows * count
+    own_heads = HEADS // count
+    images = span_starts.shape[0]
+    everything = pl.BlockSpec(memory_space=pl.ANY)
+    return pl.pallas_call(
+        functools.partial(exchange_kernel, count, images),
+        out_shape=jax.ShapeDtypeStruct(queries.shape, jnp.bfloat16),
+        in_specs=[pl.BlockSpec(memory_space=pltpu.SMEM), everything, everything, everything],
+        out_specs=everything,
+        scratch_shapes=[pltpu.VMEM((own_heads, length, HD), jnp.bfloat16)] * 4
+        + [
+            pltpu.VMEM((length, length), jnp.float32),
+            pltpu.SemaphoreType.DMA((3, own_heads, count)),
+            pltpu.SemaphoreType.DMA((3, own_heads, count)),
+            pltpu.SemaphoreType.DMA((3, own_heads)),
+            pltpu.SemaphoreType.DMA((own_heads, count)),
+            pltpu.SemaphoreType.DMA((own_heads, count)),
+            pltpu.SemaphoreType.DMA((own_heads,)),
+        ],
+        compiler_params=pltpu.CompilerParams(
+            collective_id=0, has_side_effects=True, vmem_limit_bytes=32 * 1024 * 1024
+        ),
+    )(span_starts, queries, keys, values)
+
+
 def solution(mesh):
+    count = mesh.shape["ctx"]
+    fits = count % 2 == 0 and HEADS % count == 0
+    body = functools.partial(exchange_body, count) if fits else ring_body
     placed = (P(("dp", "ctx"), None), P(("dp", "ctx"), None), P(("dp", "ctx"), None), P("dp"))
     return jax.shard_map(
         body, mesh=mesh, in_specs=placed, out_specs=P(("dp", "ctx"), None), check_vma=False

time: 114 us -> 62.3 us (0.55)
  the two profiles are of different devices: /device:TPU:16 before, /device:TPU:0 now
where the time goes in v1:
time: 62.3 us; the launch traced here: 62.1 us
  Pallas kernels  57.4 us (92%)
  local copies, waits for them, and re-layouts  4 us (6%)
  between operations  0.67 us (1%)
    pallas_call x1, Pallas kernels, exchange_body(): pl.pallas_call(functools.partial(exchange_kernel, count, images), out_sha...  57.4 us
    unnamed x7, local copies, waits for them, and re-layouts  4 us

profile of v1, /device:TPU:0, one launch (start us, length us, event | category | flops | bytes accessed | tf_op | source)
XLA Modules:
  0.0 62.1 jit_solution(12479180836465457358)
XLA Ops:
  0.7 0.0 copy-start
  0.7 1.1 %copy-done = bf16[144,2048]{1,0:T(8,128)(2,1)S(1)} copy-done((bf16[144,2048]{1,0:T(8,128)(2,1)S(1)}, bf16[144,2048]{1,0:T(8,128)(2,1)}, u32[]{:S(2)}) %copy-start) | copy-done | bytes 589848
  1.7 0.0 copy-start.1
  1.7 1.1 %copy-done.1 = bf16[144,2048]{1,0:T(8,128)(2,1)S(1)} copy-done((bf16[144,2048]{1,0:T(8,128)(2,1)S(1)}, bf16[144,2048]{1,0:T(8,128)(2,1)}, u32[]{:S(2)}) %copy-start.1) | copy-done | bytes 589848
  2.8 0.0 copy-start.2
  2.8 1.1 %copy-done.2 = bf16[144,2048]{1,0:T(8,128)(2,1)S(1)} copy-done((bf16[144,2048]{1,0:T(8,128)(2,1)S(1)}, bf16[144,2048]{1,0:T(8,128)(2,1)}, u32[]{:S(2)}) %copy-start.2) | copy-done | bytes 589848
  3.8 57.4 %shard_map.46 = bf16[144,2048]{1,0:T(8,128)(2,1)S(1)} custom-call(s32[1]{0:T(128)S(6)} %copy.6.starts_ref, bf16[144,2048]{1,0:T(8,128)(2,1)S(1)} %copy-done, bf16[144,2048]{1,0:T(8,128)(2,1)S(1)} %copy-done.1, bf16[144,2048]{1,0:T(8,128)(2,1)S(1)} %copy-done.2), custom_call_target="tpu_custom_call" | custom-call | tf_op jit(solution)/shard_map/pallas_call | solution.py:268
  61.3 0.8 %copy.7 = bf16[144,2048]{1,0:T(8,128)(2,1)} copy(bf16[144,2048]{1,0:T(8,128)(2,1)S(1)} %shard_map.46) | data formatting | bytes 1179648
Async XLA Ops:
  0.7 1.1 %copy-start = (bf16[144,2048]{1,0:T(8,128)(2,1)S(1)}, bf16[144,2048]{1,0:T(8,128)(2,1)}, u32[]{:S(2)}) copy-start(bf16[144,2048]{1,0:T(8,128)(2,1)} %q_ref.1) | copy-start | bytes 1769476
  1.7 1.1 %copy-start.1 = (bf16[144,2048]{1,0:T(8,128)(2,1)S(1)}, bf16[144,2048]{1,0:T(8,128)(2,1)}, u32[]{:S(2)}) copy-start(bf16[144,2048]{1,0:T(8,128)(2,1)} %k_ref.1) | copy-start | bytes 1769476
  2.8 1.1 %copy-start.2 = (bf16[144,2048]{1,0:T(8,128)(2,1)S(1)}, bf16[144,2048]{1,0:T(8,128)(2,1)}, u32[]{:S(2)}) copy-start(bf16[144,2048]{1,0:T(8,128)(2,1)} %v_ref.1) | copy-start | bytes 1769476

commit v2 on v1

--- a/solution.py
+++ b/solution.py
@@ -264,7 +264,7 @@
     length = rows * count
     own_heads = HEADS // count
     images = span_starts.shape[0]
-    everything = pl.BlockSpec(memory_space=pl.ANY)
+    everything = pl.BlockSpec(memory_space=pltpu.HBM)
     return pl.pallas_call(
         functools.partial(exchange_kernel, count, images),
         out_shape=jax.ShapeDtypeStruct(queries.shape, jnp.bfloat16),
@@ -281,7 +281,7 @@
             pltpu.SemaphoreType.DMA((own_heads,)),
         ],
         compiler_params=pltpu.CompilerParams(
-            collective_id=0, has_side_effects=True, vmem_limit_bytes=32 * 1024 * 1024
+            collective_id=0, has_side_effects=True, vmem_limit_bytes=56 * 1024 * 1024
         ),
     )(span_starts, queries, keys, values)
 

time: 62.3 us -> 60.6 us (0.973)
  local copies, waits for them, and re-layouts: 4 us -> 1.93 us
    unnamed x7 -> x1, local copies, waits for them, and re-layouts: 4 us -> 1.93 us
where the time goes in v2:
time: 60.6 us; the launch traced here: 60.4 us
  Pallas kernels  57.8 us (95%)
  local copies, waits for them, and re-layouts  1.93 us (3%)
  between operations  0.66 us (1%)
    pallas_call x1, Pallas kernels, exchange_body(): pl.pallas_call(functools.partial(exchange_kernel, count, images), out_sha...  57.8 us
    unnamed x1, local copies, waits for them, and re-layouts  1.93 us

profile of v2, /device:TPU:0, one launch (start us, length us, event | category | flops | bytes accessed | tf_op | source)
XLA Modules:
  0.0 60.4 jit_solution(9195752270050654216)
XLA Ops:
  0.7 57.8 %shard_map.46 = bf16[144,2048]{1,0:T(8,128)(2,1)} custom-call(s32[1]{0:T(128)S(6)} %copy.6.starts_ref, bf16[144,2048]{1,0:T(8,128)(2,1)} %q_ref.1, bf16[144,2048]{1,0:T(8,128)(2,1)} %k_ref.1, bf16[144,2048]{1,0:T(8,128)(2,1)} %v_ref.1), custom_call_target="tpu_custom_call" | custom-call | tf_op jit(solution)/shard_map/pallas_call | solution.py:268
  58.4 1.9 %copy.7 = bf16[144,2048]{1,0:T(8,128)(2,1)} copy(bf16[144,2048]{1,0:T(8,128)(2,1)} %shard_map.46) | data formatting | bytes 1179648

commit v3 on v2

--- a/solution.py
+++ b/solution.py
@@ -286,10 +286,413 @@
     )(span_starts, queries, keys, values)
 
 
+def cut_kernel(
+    starts_ref, q_ref, k_ref, v_ref, out_ref,
+    q_half, k_half, v_half, o_half, cross_in, cross_out, stat_in, stat_out,
+    bias_own, bias_low, bias_high,
+    half_send, half_recv, half_local, cross_send, cross_recv,
+    stat_send, stat_recv, out_send, out_recv, out_local,
+):
+    me = lax.axis_index("ctx")
+    rows = q_ref.shape[0]
+    pair = 2 * rows
+    steps = HEADS // 2
+    scale = HD ** (-0.5) * math.log2(math.e)
+    sources = (q_ref, k_ref, v_ref)
+    halves = (q_half, k_half, v_half)
+    first = starts_ref[0]
+    by_query = first >= rows
+    LOW, HIGH = slice(0, rows), slice(rows, pair)
+
+    def columns(head):
+        return pl.ds(pl.multiple_of(head * HD, HD), HD)
+
+    def remote(src, dst, send, recv, peer):
+        return pltpu.make_async_remote_copy(
+            src_ref=src, dst_ref=dst, send_sem=send, recv_sem=recv,
+            device_id={"ctx": peer}, device_id_type=pl.DeviceIdType.MESH,
+        )
+
+    def half_copy(which, head, part, peer):
+        return remote(
+            sources[which].at[:, columns(head)], halves[which].at[head, part, :],
+            half_send.at[which, head], half_recv.at[which, head], peer,
+        )
+
+    def own_copy(which, head, part):
+        return pltpu.make_async_copy(
+            sources[which].at[:, columns(head)], halves[which].at[head, part, :],
+            half_local.at[which, head],
+        )
+
+    def cross_copy(slot, step, peer):
+        return remote(
+            cross_out.at[slot, step], cross_in.at[slot, step],
+            cross_send.at[slot, step], cross_recv.at[slot, step], peer,
+        )
+
+    def query_copy(step, peer):
+        return remote(
+            q_half.at[step], cross_in.at[0, step],
+            cross_send.at[0, step], cross_recv.at[0, step], peer,
+        )
+
+    def stat_copy(step, peer):
+        return remote(
+            stat_out.at[step], stat_in.at[step], stat_send.at[step], stat_recv.at[step], peer
+        )
+
+    def result_copy(head, part, peer):
+        return remote(
+            o_half.at[head, part, :], out_ref.at[:, columns(head)],
+            out_send.at[head], out_recv.at[head], peer,
+        )
+
+    def result_local(head, part):
+        return pltpu.make_async_copy(
+            o_half.at[head, part, :], out_ref.at[:, columns(head)], out_local.at[head]
+        )
+
+    def scores_of(query, key):
+        return lax.dot_general(
+            query, key, (((1,), (1,)), ((), ())), preferred_element_type=jnp.float32
+        ) * scale
+
+    def weigh(scores, top):
+        return jnp.exp2(scores - top)
+
+    def mix(weights, value):
+        return jnp.dot(weights.astype(jnp.bfloat16), value, preferred_element_type=jnp.float32)
+
+    def attend(query, key, value, bias=None):
+        scores = scores_of(query, key)
+        if bias is not None:
+            scores = scores + bias
+        top = jnp.max(scores, axis=1, keepdims=True)
+        weights = weigh(scores, top)
+        return mix(weights, value), top, jnp.sum(weights, axis=1, keepdims=True)
+
+    def as_row(column):
+        return jnp.transpose(jnp.broadcast_to(column, (pair, HD)))[0:1, :]
+
+    def as_columns(row):
+        return jnp.transpose(jnp.broadcast_to(row, (HD, pair)))
+
+    def merge(mixed, top, total, other, other_log):
+        peak = jnp.maximum(top, other_log)
+        mine, theirs = jnp.exp2(top - peak), jnp.exp2(other_log - peak)
+        return (mixed * mine + other * theirs) / (total * mine + theirs)
+
+    def hidden(query_start, query_rows, key_start, key_rows, causal):
+        query_pos = query_start + lax.broadcasted_iota(jnp.int32, (query_rows, key_rows), 0)
+        key_pos = key_start + lax.broadcasted_iota(jnp.int32, (query_rows, key_rows), 1)
+        visible = (
+            (query_pos >= first) & (query_pos < first + SPAN)
+            & (key_pos >= first) & (key_pos < first + SPAN)
+        )
+        if causal:
+            visible = visible | (key_pos <= query_pos)
+        return jnp.where(visible, 0.0, -1e30)
+
+    barrier = pltpu.get_barrier_semaphore()
+
+    @pl.when(me > 0)
+    def _():
+        pl.semaphore_signal(
+            barrier, inc=1, device_id={"ctx": me - 1}, device_id_type=pl.DeviceIdType.MESH
+        )
+
+    @pl.when(me < 3)
+    def _():
+        pl.semaphore_signal(
+            barrier, inc=1, device_id={"ctx": me + 1}, device_id_type=pl.DeviceIdType.MESH
+        )
+
+    @pl.when((me == 0) | (me == 3))
+    def _():
+        pl.semaphore_wait(barrier, 1)
+
+    @pl.when((me == 1) | (me == 2))
+    def _():
+        pl.semaphore_wait(barrier, 2)
+
+    def repeat(count, one):
+        lax.fori_loop(0, count, lambda step, carry: (one(step), carry)[1], 0)
+
+    def outer_end(part, peer):
+        def one(head):
+            for which in range(3):
+                half_copy(which, head, part, peer).wait_send()
+            result_copy(head, part, peer).wait_recv()
+
+        repeat(HEADS, one)
+
+    @pl.when(me == 0)
+    def _():
+        def first_part(step):
+            half_copy(1, steps + step, LOW, me + 1).start()
+            half_copy(1, step, LOW, me + 1).start()
+            half_copy(2, step, LOW, me + 1).start()
+
+        repeat(steps, first_part)
+        repeat(steps, lambda step: half_copy(2, steps + step, LOW, me + 1).start())
+        repeat(HEADS, lambda head: half_copy(0, head, LOW, me + 1).start())
+        outer_end(LOW, me + 1)
+
+    @pl.when(me == 3)
+    def _():
+        repeat(HEADS, lambda head: half_copy(0, head, HIGH, me - 1).start())
+
+        def pair_part(head):
+            half_copy(1, head, HIGH, me - 1).start()
+            half_copy(2, head, HIGH, me - 1).start()
+
+        repeat(HEADS, pair_part)
+        outer_end(HIGH, me - 1)
+
+    def own_start(part):
+        def one(head):
+            for which in range(3):
+                own_copy(which, head, part).start()
+
+        repeat(HEADS, one)
+
+    def own_wait(part):
+        def one(head):
+            for which in range(3):
+                own_copy(which, head, part).wait()
+
+        repeat(HEADS, one)
+
+    @pl.when(me == 1)
+    def _():
+        peer, outer = me + 1, me - 1
+        own_start(HIGH)
+        bias_own[...] = hidden(0, pair, 0, pair, True)
+        bias_low[...] = jnp.where(by_query, -1e30, hidden(0, pair, pair, rows, False))
+        own_wait(HIGH)
+
+        def arrived(which, head):
+            half_copy(which, head, LOW, outer).wait_recv()
+
+        def first_part(step):
+            arrived(1, steps + step)
+            for side, part in enumerate((LOW, HIGH)):
+                cross_out[1, step, part, :] = jnp.where(
+                    by_query, q_half[2 * step + side, HIGH, :], k_half[steps + step, part, :]
+                )
+            cross_copy(1, step, peer).start()
+            arrived(1, step)
+            arrived(2, step)
+            query_copy(step, peer).wait_recv()
+            mixed, top, total = attend(cross_in[0, step], k_half[step], v_half[step])
+            cross_out[0, step] = (mixed / total).astype(jnp.bfloat16)
+            stat_out[step] = as_row(top + jnp.log2(total))
+            cross_copy(0, step, peer).start()
+            stat_copy(step, peer).start()
+
+        repeat(steps, first_part)
+
+        def second_part(step):
+            arrived(2, steps + step)
+            cross_copy(1, step, peer).wait_recv()
+            mixed, top, total = attend(
+                cross_in[1, step], k_half[steps + step], v_half[steps + step]
+            )
+            cross_out[2, step] = jnp.where(
+                by_query, (mixed / total).astype(jnp.bfloat16), v_half[steps + step]
+            )
+            stat_out[steps + step] = as_row(top + jnp.log2(total))
+            cross_copy(2, step, peer).start()
+            stat_copy(steps + step, peer).start()
+
+        repeat(steps, second_part)
+
+        def third_part(step):
+            cross_copy(2, step, peer).wait_recv()
+            stat_copy(step, peer).wait_recv()
+            logs = as_columns(jnp.where(by_query, stat_in[step], -1e30))
+            for side, part in enumerate((LOW, HIGH)):
+                head = 2 * step + side
+                arrived(0, head)
+                query = q_half[head]
+                near = scores_of(query, k_half[head]) + bias_own[...]
+                far = scores_of(query, cross_in[1, step, part, :]) + bias_low[...]
+                top = jnp.maximum(
+                    jnp.max(near, axis=1, keepdims=True), jnp.max(far, axis=1, keepdims=True)
+                )
+                near, far = weigh(near, top), weigh(far, top)
+                total = jnp.sum(near, axis=1, keepdims=True) + jnp.sum(
+                    far, axis=1, keepdims=True
+                )
+                other = cross_in[2, step, part, :]
+                mixed = mix(near, v_half[head]) + mix(far, other)
+                o_half[head, LOW, :] = (mixed[LOW] / total[LOW]).astype(jnp.bfloat16)
+                o_half[head, HIGH, :] = merge(
+                    mixed[HIGH], top[HIGH], total[HIGH],
+                    other.astype(jnp.float32), logs[part],
+                ).astype(jnp.bfloat16)
+                result_copy(head, LOW, outer).start()
+                result_local(head, HIGH).start()
+
+        repeat(steps, third_part)
+
+        def finish(step):
+            for slot in range(3):
+                cross_copy(slot, step, peer).wait_send()
+            for side in range(2):
+                stat_copy(2 * step + side, peer).wait_send()
+                result_copy(2 * step + side, LOW, outer).wait_send()
+                result_local(2 * step + side, HIGH).wait()
+
+        repeat(steps, finish)
+
+    @pl.when(me == 2)
+    def _():
+        peer, outer = me - 1, me + 1
+        own_start(LOW)
+        bias_own[...] = hidden(pair, pair, pair, pair, True)
+        bias_high[...] = hidden(rows, rows, pair, pair, False)
+        own_wait(LOW)
+
+        def arrived(which, head):
+            half_copy(which, head, HIGH, outer).wait_recv()
+
+        def send_query(step):
+            arrived(0, step)
+            query_copy(step, peer).start()
+
+        repeat(steps, send_query)
+
+        def send_either(step):
+            arrived(0, steps + step)
+            for side, part in enumerate((LOW, HIGH)):
+                cross_out[1, step, part, :] = jnp.where(
+                    by_query, q_half[steps + step, part, :], k_half[2 * step + side, LOW, :]
+                )
+            cross_copy(1, step, peer).start()
+
+        repeat(steps, send_either)
+
+        def send_span(step):
+            cross_copy(1, step, peer).wait_recv()
+            tops, totals = [], []
+            for side, part in enumerate((LOW, HIGH)):
+                head = 2 * step + side
+                arrived(1, head)
+                arrived(2, head)
+                mixed, top, total = attend(
+                    cross_in[1, step, part, :], k_half[head], v_half[head], bias_high[...]
+                )
+                cross_out[2, step, part, :] = jnp.where(
+                    by_query, (mixed / total).astype(jnp.bfloat16), v_half[head, LOW, :]
+                )
+                tops.append(top)
+                totals.append(total)
+            logs = jnp.concatenate(tops, axis=0) + jnp.log2(jnp.concatenate(totals, axis=0))
+            stat_out[step] = as_row(logs)
+            cross_copy(2, step, peer).start()
+            stat_copy(step, peer).start()
+
+        def give(head, mixed, top, total, other, logs):
+            o_half[head] = merge(mixed, top, total, other, logs).astype(jnp.bfloat16)
+            result_copy(head, HIGH, outer).start()
+            result_local(head, LOW).start()
+
+        def finish_low(step):
+            cross_copy(0, step, peer).wait_recv()
+            stat_copy(step, peer).wait_recv()
+            mixed, top, total = attend(
+                q_half[step], k_half[step], v_half[step], bias_own[...]
+            )
+            other = cross_in[0, step].astype(jnp.float32)
+            give(step, mixed, top, total, other, as_columns(stat_in[step]))
+
+        def finish_high(step):
+            head = steps + step
+            cross_copy(2, step, peer).wait_recv()
+            stat_copy(head, peer).wait_recv()
+            mixed, top, total = attend(
+                q_half[head], k_half[head], v_half[head], bias_own[...]
+            )
+            low_mixed, low_top, low_total = attend(
+                q_half[head], cross_in[1, step], cross_in[2, step]
+            )
+            other = jnp.where(
+                by_query, cross_in[2, step].astype(jnp.float32), low_mixed / low_total
+            )
+            logs = jnp.where(
+                by_query, as_columns(stat_in[head]),
+                jnp.broadcast_to(low_top + jnp.log2(low_total), (pair, HD)),
+            )
+            give(head, mixed, top, total, other, logs)
+
+        def both(step):
+            send_span(step)
+            finish_low(step)
+
+        repeat(steps // 2, both)
+
+        def late(step):
+            send_span(steps // 2 + step)
+            finish_low(steps // 2 + step)
+            finish_high(2 * step)
+            finish_high(2 * step + 1)
+
+        repeat(steps // 2, late)
+
+        def finish(step):
+            query_copy(step, peer).wait_send()
+            for slot in (1, 2):
+                cross_copy(slot, step, peer).wait_send()
+            stat_copy(step, peer).wait_send()
+            for side in range(2):
+                result_copy(2 * step + side, HIGH, outer).wait_send()
+                result_local(2 * step + side, LOW).wait()
+
+        repeat(steps, finish)
+
+
+def cut_body(queries, keys, values, span_starts):
+    rows = queries.shape[0]
+    pair = 2 * rows
+    steps = HEADS // 2
+    everything = pl.BlockSpec(memory_space=pltpu.HBM)
+    dma = pltpu.SemaphoreType.DMA
+    return pl.pallas_call(
+        cut_kernel,
+        out_shape=jax.ShapeDtypeStruct(queries.shape, jnp.bfloat16),
+        in_specs=[pl.BlockSpec(memory_space=pltpu.SMEM), everything, everything, everything],
+        out_specs=everything,
+        scratch_shapes=[pltpu.VMEM((HEADS, pair, HD), jnp.bfloat16)] * 4
+        + [pltpu.VMEM((3, steps, pair, HD), jnp.bfloat16)] * 2
+        + [pltpu.VMEM((HEADS, 1, pair), jnp.float32)] * 2
+        + [
+            pltpu.VMEM((pair, pair), jnp.float32),
+            pltpu.VMEM((pair, rows), jnp.float32),
+            pltpu.VMEM((rows, pair), jnp.float32),
+            dma((3, HEADS)), dma((3, HEADS)), dma((3, HEADS)),
+            dma((3, steps)), dma((3, steps)),
+            dma((HEADS,)), dma((HEADS,)),
+            dma((HEADS,)), dma((HEADS,)), dma((HEADS,)),
+        ],
+        compiler_params=pltpu.CompilerParams(
+            collective_id=0, has_side_effects=True, vmem_limit_bytes=56 * 1024 * 1024
+        ),
+    )(span_starts, queries, keys, values)
+
+
+def chosen_body(count, queries, keys, values, span_starts):
+    rows, images = queries.shape[0], span_starts.shape[0]
+    if count == 4 and images == 1 and SPAN <= 2 * rows and rows % 16 == 0:
+        return cut_body(queries, keys, values, span_starts)
+    if count % 2 == 0 and HEADS % count == 0:
+        return exchange_body(count, queries, keys, values, span_starts)
+    return ring_body(queries, keys, values, span_starts)
+
+
 def solution(mesh):
-    count = mesh.shape["ctx"]
-    fits = count % 2 == 0 and HEADS % count == 0
-    body = functools.partial(exchange_body, count) if fits else ring_body
+    body = functools.partial(chosen_body, mesh.shape["ctx"])
     placed = (P(("dp", "ctx"), None), P(("dp", "ctx"), None), P(("dp", "ctx"), None), P("dp"))
     return jax.shard_map(
         body, mesh=mesh, in_specs=placed, out_specs=P(("dp", "ctx"), None), check_vma=False

time: 60.6 us -> 62.9 us (1.038)
  Pallas kernels: 57.8 us -> 60 us
    pallas_call x1, Pallas kernels: 57.8 us -> 60 us  [cut_body(): pl.pallas_call(cut_kernel, out_shape=jax.ShapeDtypeStruct(queries.shape,...]
where the time goes in v3:
time: 62.9 us; the launch traced here: 62.6 us
  Pallas kernels  60 us (95%)
  local copies, waits for them, and re-layouts  1.93 us (3%)
  between operations  0.66 us (1%)
    pallas_call x1, Pallas kernels, cut_body(): pl.pallas_call(cut_kernel, out_shape=jax.ShapeDtypeStruct(queries.shape,...  60 us
    unnamed x1, local copies, waits for them, and re-layouts  1.93 us

profile of v3, /device:TPU:0, one launch (start us, length us, event | category | flops | bytes accessed | tf_op | source)
XLA Modules:
  0.0 62.6 jit_solution(7776677336457389648)
XLA Ops:
  0.7 60.0 %shard_map.46 = bf16[144,2048]{1,0:T(8,128)(2,1)} custom-call(s32[1]{0:T(128)S(6)} %copy.6.starts_ref, bf16[144,2048]{1,0:T(8,128)(2,1)} %q_ref.1, bf16[144,2048]{1,0:T(8,128)(2,1)} %k_ref.1, bf16[144,2048]{1,0:T(8,128)(2,1)} %v_ref.1), custom_call_target="tpu_custom_call" | custom-call | tf_op jit(solution)/shard_map/pallas_call | solution.py:662
  60.7 1.9 %copy.7 = bf16[144,2048]{1,0:T(8,128)(2,1)} copy(bf16[144,2048]{1,0:T(8,128)(2,1)} %shard_map.46) | data formatting | bytes 1179648

commit v4 on v3

--- a/solution.py
+++ b/solution.py
@@ -364,13 +364,16 @@
     def mix(weights, value):
         return jnp.dot(weights.astype(jnp.bfloat16), value, preferred_element_type=jnp.float32)
 
-    def attend(query, key, value, bias=None):
-        scores = scores_of(query, key)
-        if bias is not None:
-            scores = scores + bias
-        top = jnp.max(scores, axis=1, keepdims=True)
-        weights = weigh(scores, top)
-        return mix(weights, value), top, jnp.sum(weights, axis=1, keepdims=True)
+    def attend(items):
+        scores = [
+            scores_of(query, key) if bias is None else scores_of(query, key) + bias
+            for query, key, value, bias in items
+        ]
+        tops = [jnp.max(score, axis=1, keepdims=True) for score in scores]
+        weights = [weigh(score, top) for score, top in zip(scores, tops)]
+        totals = [jnp.sum(weight, axis=1, keepdims=True) for weight in weights]
+        mixed = [mix(weight, item[2]) for weight, item in zip(weights, items)]
+        return list(zip(mixed, tops, totals))
 
     def as_row(column):
         return jnp.transpose(jnp.broadcast_to(column, (pair, HD)))[0:1, :]
@@ -475,63 +478,86 @@
         def arrived(which, head):
             half_copy(which, head, LOW, outer).wait_recv()
 
-        def first_part(step):
-            arrived(1, steps + step)
-            for side, part in enumerate((LOW, HIGH)):
-                cross_out[1, step, part, :] = jnp.where(
-                    by_query, q_half[2 * step + side, HIGH, :], k_half[steps + step, part, :]
+        def first_part(turn):
+            both = (2 * turn, 2 * turn + 1)
+            for step in both:
+                arrived(1, steps + step)
+                for side, part in enumerate((LOW, HIGH)):
+                    cross_out[1, step, part, :] = jnp.where(
+                        by_query, q_half[2 * step + side, HIGH, :], k_half[steps + step, part, :]
+                    )
+                cross_copy(1, step, peer).start()
+            for step in both:
+                arrived(1, step)
+                arrived(2, step)
+                query_copy(step, peer).wait_recv()
+            done = attend([(cross_in[0, step], k_half[step], v_half[step], None) for step in both])
+            for step, (mixed, top, total) in zip(both, done):
+                cross_out[0, step] = (mixed / total).astype(jnp.bfloat16)
+                stat_out[step] = as_row(top + jnp.log2(total))
+            for step in both:
+                cross_copy(0, step, peer).start()
+                stat_copy(step, peer).start()
+
+        repeat(steps // 2, first_part)
+
+        def second_part(turn):
+            both = (2 * turn, 2 * turn + 1)
+            for step in both:
+                arrived(2, steps + step)
+                cross_copy(1, step, peer).wait_recv()
+            done = attend([
+                (cross_in[1, step], k_half[steps + step], v_half[steps + step], None)
+                for step in both
+            ])
+            for step, (mixed, top, total) in zip(both, done):
+                cross_out[2, step] = jnp.where(
+                    by_query, (mixed / total).astype(jnp.bfloat16), v_half[steps + step]
                 )
-            cross_copy(1, step, peer).start()
-            arrived(1, step)
-            arrived(2, step)
-            query_copy(step, peer).wait_recv()
-            mixed, top, total = attend(cross_in[0, step], k_half[step], v_half[step])
-            cross_out[0, step] = (mixed / total).astype(jnp.bfloat16)
-            stat_out[step] = as_row(top + jnp.log2(total))
-            cross_copy(0, step, peer).start()
-            stat_copy(step, peer).start()
-
-        repeat(steps, first_part)
-
-        def second_part(step):
-            arrived(2, steps + step)
-            cross_copy(1, step, peer).wait_recv()
-            mixed, top, total = attend(
-                cross_in[1, step], k_half[steps + step], v_half[steps + step]
-            )
-            cross_out[2, step] = jnp.where(
-                by_query, (mixed / total).astype(jnp.bfloat16), v_half[steps + step]
-            )
-            stat_out[steps + step] = as_row(top + jnp.log2(total))
-            cross_copy(2, step, peer).start()
-            stat_copy(steps + step, peer).start()
-
-        repeat(steps, second_part)
+                stat_out[steps + step] = as_row(top + jnp.log2(total))
+            for step in both:
+                cross_copy(2, step, peer).start()
+                stat_copy(steps + step, peer).start()
+
+        repeat(steps // 2, second_part)
 
         def third_part(step):
+            heads = (2 * step, 2 * step + 1)
+            parts = (LOW, HIGH)
             cross_copy(2, step, peer).wait_recv()
             stat_copy(step, peer).wait_recv()
+            for head in heads:
+                arrived(0, head)
             logs = as_columns(jnp.where(by_query, stat_in[step], -1e30))
-            for side, part in enumerate((LOW, HIGH)):
-                head = 2 * step + side
-                arrived(0, head)
-                query = q_half[head]
-                near = scores_of(query, k_half[head]) + bias_own[...]
-                far = scores_of(query, cross_in[1, step, part, :]) + bias_low[...]
-                top = jnp.maximum(
-                    jnp.max(near, axis=1, keepdims=True), jnp.max(far, axis=1, keepdims=True)
-                )
-                near, far = weigh(near, top), weigh(far, top)
-                total = jnp.sum(near, axis=1, keepdims=True) + jnp.sum(
-                    far, axis=1, keepdims=True
-                )
-                other = cross_in[2, step, part, :]
-                mixed = mix(near, v_half[head]) + mix(far, other)
+            near = [scores_of(q_half[head], k_half[head]) + bias_own[...] for head in heads]
+            far = [
+                scores_of(q_half[head], cross_in[1, step, part, :]) + bias_low[...]
+                for head, part in zip(heads, parts)
+            ]
+            tops = [
+                jnp.maximum(jnp.max(a, axis=1, keepdims=True), jnp.max(b, axis=1, keepdims=True))
+                for a, b in zip(near, far)
+            ]
+            near = [weigh(score, top) for score, top in zip(near, tops)]
+            far = [weigh(score, top) for score, top in zip(far, tops)]
+            totals = [
+                jnp.sum(a, axis=1, keepdims=True) + jnp.sum(b, axis=1, keepdims=True)
+                for a, b in zip(near, far)
+            ]
+            others = [cross_in[2, step, part, :] for part in parts]
+            mixes = [
+                mix(a, v_half[head]) + mix(b, other)
+                for a, b, head, other in zip(near, far, heads, others)
+            ]
+            for head, part, mixed, top, total, other in zip(
+                heads, parts, mixes, tops, totals, others
+            ):
                 o_half[head, LOW, :] = (mixed[LOW] / total[LOW]).astype(jnp.bfloat16)
                 o_half[head, HIGH, :] = merge(
                     mixed[HIGH], top[HIGH], total[HIGH],
                     other.astype(jnp.float32), logs[part],
                 ).astype(jnp.bfloat16)
+            for head in heads:
                 result_copy(head, LOW, outer).start()
                 result_local(head, HIGH).start()
 
@@ -574,72 +600,78 @@
 
         repeat(steps, send_either)
 
-        def send_span(step):
+        def give(heads):
+            for head in heads:
+                result_copy(head, HIGH, outer).start()
+                result_local(head, LOW).start()
+
+        def span_and_low(step):
+            heads = (2 * step, 2 * step + 1)
+            parts = (LOW, HIGH)
             cross_copy(1, step, peer).wait_recv()
-            tops, totals = [], []
-            for side, part in enumerate((LOW, HIGH)):
-                head = 2 * step + side
+            for head in heads:
                 arrived(1, head)
                 arrived(2, head)
-                mixed, top, total = attend(
-                    cross_in[1, step, part, :], k_half[head], v_half[head], bias_high[...]
-                )
+            cross_copy(0, step, peer).wait_recv()
+            stat_copy(step, peer).wait_recv()
+            done = attend(
+                [
+                    (cross_in[1, step, part, :], k_half[head], v_half[head], bias_high[...])
+                    for head, part in zip(heads, parts)
+                ]
+                + [(q_half[step], k_half[step], v_half[step], bias_own[...])]
+            )
+            for head, part, (mixed, top, total) in zip(heads, parts, done):
                 cross_out[2, step, part, :] = jnp.where(
                     by_query, (mixed / total).astype(jnp.bfloat16), v_half[head, LOW, :]
                 )
-                tops.append(top)
-                totals.append(total)
-            logs = jnp.concatenate(tops, axis=0) + jnp.log2(jnp.concatenate(totals, axis=0))
-            stat_out[step] = as_row(logs)
+            stat_out[step] = as_row(
+                jnp.concatenate([top + jnp.log2(total) for mixed, top, total in done[:2]], axis=0)
+            )
+            mixed, top, total = done[2]
+            o_half[step] = merge(
+                mixed, top, total, cross_in[0, step].astype(jnp.float32),
+                as_columns(stat_in[step]),
+            ).astype(jnp.bfloat16)
             cross_copy(2, step, peer).start()
             stat_copy(step, peer).start()
-
-        def give(head, mixed, top, total, other, logs):
-            o_half[head] = merge(mixed, top, total, other, logs).astype(jnp.bfloat16)
-            result_copy(head, HIGH, outer).start()
-            result_local(head, LOW).start()
-
-        def finish_low(step):
-            cross_copy(0, step, peer).wait_recv()
-            stat_copy(step, peer).wait_recv()
-            mixed, top, total = attend(
-                q_half[step], k_half[step], v_half[step], bias_own[...]
+            give((step,))
+
+        def high_pair(turn):
+            both = (2 * turn, 2 * turn + 1)
+            for step in both:
+                cross_copy(2, step, peer).wait_recv()
+                stat_copy(steps + step, peer).wait_recv()
+            done = attend(
+                [
+                    (q_half[steps + step], k_half[steps + step], v_half[steps + step], bias_own[...])
+                    for step in both
+                ]
+                + [
+                    (q_half[steps + step], cross_in[1, step], cross_in[2, step], None)
+                    for step in both
+                ]
             )
-            other = cross_in[0, step].astype(jnp.float32)
-            give(step, mixed, top, total, other, as_columns(stat_in[step]))
-
-        def finish_high(step):
-            head = steps + step
-            cross_copy(2, step, peer).wait_recv()
-            stat_copy(head, peer).wait_recv()
-            mixed, top, total = attend(
-                q_half[head], k_half[head], v_half[head], bias_own[...]
-            )
-            low_mixed, low_top, low_total = attend(
-                q_half[head], cross_in[1, step], cross_in[2, step]
-            )
-            other = jnp.where(
-                by_query, cross_in[2, step].astype(jnp.float32), low_mixed / low_total
-            )
-            logs = jnp.where(
-                by_query, as_columns(stat_in[head]),
-                jnp.broadcast_to(low_top + jnp.log2(low_total), (pair, HD)),
-            )
-            give(head, mixed, top, total, other, logs)
-
-        def both(step):
-            send_span(step)
-            finish_low(step)
-
-        repeat(steps // 2, both)
-
-        def late(step):
-            send_span(steps // 2 + step)
-            finish_low(steps // 2 + step)
-            finish_high(2 * step)
-            finish_high(2 * step + 1)
-
-        repeat(steps // 2, late)
+            for step, near, low in zip(both, done[:2], done[2:]):
+                other = jnp.where(
+                    by_query, cross_in[2, step].astype(jnp.float32), low[0] / low[2]
+                )
+                logs = jnp.where(
+                    by_query, as_columns(stat_in[steps + step]),
+                    jnp.broadcast_to(low[1] + jnp.log2(low[2]), (pair, HD)),
+                )
+                o_half[steps + step] = merge(*near, other, logs).astype(jnp.bfloat16)
+            give([steps + step for step in both])
+
+        early = steps // 2 + 1
+        repeat(early, span_and_low)
+
+        def late(turn):
+            span_and_low(early + turn)
+            high_pair(turn)
+
+        repeat(steps - early, late)
+        high_pair(steps - early)
 
         def finish(step):
             query_copy(step, peer).wait_send()
@@ -663,7 +695,7 @@
         cut_kernel,
         out_shape=jax.ShapeDtypeStruct(queries.shape, jnp.bfloat16),
         in_specs=[pl.BlockSpec(memory_space=pltpu.SMEM), everything, everything, everything],
-        out_specs=everything,
+        out_specs=pl.BlockSpec(memory_space=pl.ANY),
         scratch_shapes=[pltpu.VMEM((HEADS, pair, HD), jnp.bfloat16)] * 4
         + [pltpu.VMEM((3, steps, pair, HD), jnp.bfloat16)] * 2
         + [pltpu.VMEM((HEADS, 1, pair), jnp.float32)] * 2
@@ -677,7 +709,7 @@
             dma((HEADS,)), dma((HEADS,)), dma((HEADS,)),
         ],
         compiler_params=pltpu.CompilerParams(
-            collective_id=0, has_side_effects=True, vmem_limit_bytes=56 * 1024 * 1024
+            collective_id=0, has_side_effects=True, vmem_limit_bytes=32 * 1024 * 1024
         ),
     )(span_starts, queries, keys, values)
 

time: 62.9 us -> 60.8 us (0.967)
  Pallas kernels: 60 us -> 55.9 us
  local copies, waits for them, and re-layouts: 1.93 us -> 4 us
    pallas_call x1, Pallas kernels: 60 us -> 55.9 us  [cut_body(): pl.pallas_call(cut_kernel, out_shape=jax.ShapeDtypeStruct(queries.shape,...]
    unnamed x1 -> x7, local copies, waits for them, and re-layouts: 1.93 us -> 4 us
where the time goes in v4:
time: 60.8 us; the launch traced here: 60.5 us
  Pallas kernels  55.9 us (92%)
  local copies, waits for them, and re-layouts  4 us (7%)
  between operations  0.67 us (1%)
    pallas_call x1, Pallas kernels, cut_body(): pl.pallas_call(cut_kernel, out_shape=jax.ShapeDtypeStruct(queries.shape,...  55.9 us
    unnamed x7, local copies, waits for them, and re-layouts  4 us

profile of v4, /device:TPU:0, one launch (start us, length us, event | category | flops | bytes accessed | tf_op | source)
XLA Modules:
  0.0 60.5 jit_solution(14820398486305029017)
XLA Ops:
  0.7 0.0 copy-start
  0.7 1.1 %copy-done = bf16[144,2048]{1,0:T(8,128)(2,1)S(1)} copy-done((bf16[144,2048]{1,0:T(8,128)(2,1)S(1)}, bf16[144,2048]{1,0:T(8,128)(2,1)}, u32[]{:S(2)}) %copy-start) | copy-done | bytes 589848
  1.7 0.0 copy-start.1
  1.7 1.1 %copy-done.1 = bf16[144,2048]{1,0:T(8,128)(2,1)S(1)} copy-done((bf16[144,2048]{1,0:T(8,128)(2,1)S(1)}, bf16[144,2048]{1,0:T(8,128)(2,1)}, u32[]{:S(2)}) %copy-start.1) | copy-done | bytes 589848
  2.8 0.0 copy-start.2
  2.8 1.1 %copy-done.2 = bf16[144,2048]{1,0:T(8,128)(2,1)S(1)} copy-done((bf16[144,2048]{1,0:T(8,128)(2,1)S(1)}, bf16[144,2048]{1,0:T(8,128)(2,1)}, u32[]{:S(2)}) %copy-start.2) | copy-done | bytes 589848
  3.8 55.9 %shard_map.46 = bf16[144,2048]{1,0:T(8,128)(2,1)S(1)} custom-call(s32[1]{0:T(128)S(6)} %copy.6.starts_ref, bf16[144,2048]{1,0:T(8,128)(2,1)S(1)} %copy-done, bf16[144,2048]{1,0:T(8,128)(2,1)S(1)} %copy-done.1, bf16[144,2048]{1,0:T(8,128)(2,1)S(1)} %copy-done.2), custom_call_target="tpu_custom_call" | custom-call | tf_op jit(solution)/shard_map/pallas_call | solution.py:694
  59.7 0.8 %copy.7 = bf16[144,2048]{1,0:T(8,128)(2,1)} copy(bf16[144,2048]{1,0:T(8,128)(2,1)S(1)} %shard_map.46) | data formatting | bytes 1179648
Async XLA Ops:
  0.7 1.1 %copy-start = (bf16[144,2048]{1,0:T(8,128)(2,1)S(1)}, bf16[144,2048]{1,0:T(8,128)(2,1)}, u32[]{:S(2)}) copy-start(bf16[144,2048]{1,0:T(8,128)(2,1)} %q_ref.1) | copy-start | bytes 1769476
  1.7 1.1 %copy-start.1 = (bf16[144,2048]{1,0:T(8,128)(2,1)S(1)}, bf16[144,2048]{1,0:T(8,128)(2,1)}, u32[]{:S(2)}) copy-start(bf16[144,2048]{1,0:T(8,128)(2,1)} %k_ref.1) | copy-start | bytes 1769476
  2.8 1.1 %copy-start.2 = (bf16[144,2048]{1,0:T(8,128)(2,1)S(1)}, bf16[144,2048]{1,0:T(8,128)(2,1)}, u32[]{:S(2)}) copy-start(bf16[144,2048]{1,0:T(8,128)(2,1)} %v_ref.1) | copy-start | bytes 1769476

commit v5 on v4

--- a/solution.py
+++ b/solution.py
@@ -433,10 +433,10 @@
     @pl.when(me == 0)
     def _():
         def first_part(step):
-            half_copy(1, steps + step, LOW, me + 1).start()
             half_copy(1, step, LOW, me + 1).start()
             half_copy(2, step, LOW, me + 1).start()
 
+        repeat(steps, lambda step: half_copy(1, steps + step, LOW, me + 1).start())
         repeat(steps, first_part)
         repeat(steps, lambda step: half_copy(2, steps + step, LOW, me + 1).start())
         repeat(HEADS, lambda head: half_copy(0, head, LOW, me + 1).start())
@@ -478,15 +478,18 @@
         def arrived(which, head):
             half_copy(which, head, LOW, outer).wait_recv()
 
+        def send_either(step):
+            arrived(1, steps + step)
+            for side, part in enumerate((LOW, HIGH)):
+                cross_out[1, step, part, :] = jnp.where(
+                    by_query, q_half[2 * step + side, HIGH, :], k_half[steps + step, part, :]
+                )
+            cross_copy(1, step, peer).start()
+
+        repeat(steps, send_either)
+
         def first_part(turn):
             both = (2 * turn, 2 * turn + 1)
-            for step in both:
-                arrived(1, steps + step)
-                for side, part in enumerate((LOW, HIGH)):
-                    cross_out[1, step, part, :] = jnp.where(
-                        by_query, q_half[2 * step + side, HIGH, :], k_half[steps + step, part, :]
-                    )
-                cross_copy(1, step, peer).start()
             for step in both:
                 arrived(1, step)
                 arrived(2, step)
@@ -524,38 +527,27 @@
         def third_part(step):
             heads = (2 * step, 2 * step + 1)
             parts = (LOW, HIGH)
+            for head in heads:
+                arrived(0, head)
+            near = attend([
+                (q_half[head], k_half[head], v_half[head], bias_own[...]) for head in heads
+            ])
             cross_copy(2, step, peer).wait_recv()
             stat_copy(step, peer).wait_recv()
-            for head in heads:
-                arrived(0, head)
             logs = as_columns(jnp.where(by_query, stat_in[step], -1e30))
-            near = [scores_of(q_half[head], k_half[head]) + bias_own[...] for head in heads]
-            far = [
-                scores_of(q_half[head], cross_in[1, step, part, :]) + bias_low[...]
+            far = attend([
+                (q_half[head], cross_in[1, step, part, :], cross_in[2, step, part, :], bias_low[...])
                 for head, part in zip(heads, parts)
-            ]
-            tops = [
-                jnp.maximum(jnp.max(a, axis=1, keepdims=True), jnp.max(b, axis=1, keepdims=True))
-                for a, b in zip(near, far)
-            ]
-            near = [weigh(score, top) for score, top in zip(near, tops)]
-            far = [weigh(score, top) for score, top in zip(far, tops)]
-            totals = [
-                jnp.sum(a, axis=1, keepdims=True) + jnp.sum(b, axis=1, keepdims=True)
-                for a, b in zip(near, far)
-            ]
-            others = [cross_in[2, step, part, :] for part in parts]
-            mixes = [
-                mix(a, v_half[head]) + mix(b, other)
-                for a, b, head, other in zip(near, far, heads, others)
-            ]
-            for head, part, mixed, top, total, other in zip(
-                heads, parts, mixes, tops, totals, others
-            ):
+            ])
+            for head, part, own, span in zip(heads, parts, near, far):
+                top = jnp.maximum(own[1], span[1])
+                mine, theirs = jnp.exp2(own[1] - top), jnp.exp2(span[1] - top)
+                mixed = own[0] * mine + span[0] * theirs
+                total = own[2] * mine + span[2] * theirs
                 o_half[head, LOW, :] = (mixed[LOW] / total[LOW]).astype(jnp.bfloat16)
                 o_half[head, HIGH, :] = merge(
                     mixed[HIGH], top[HIGH], total[HIGH],
-                    other.astype(jnp.float32), logs[part],
+                    cross_in[2, step, part, :].astype(jnp.float32), logs[part],
                 ).astype(jnp.bfloat16)
             for head in heads:
                 result_copy(head, LOW, outer).start()
@@ -612,55 +604,50 @@
             for head in heads:
                 arrived(1, head)
                 arrived(2, head)
-            cross_copy(0, step, peer).wait_recv()
-            stat_copy(step, peer).wait_recv()
-            done = attend(
-                [
-                    (cross_in[1, step, part, :], k_half[head], v_half[head], bias_high[...])
-                    for head, part in zip(heads, parts)
-                ]
-                + [(q_half[step], k_half[step], v_half[step], bias_own[...])]
-            )
+            done = attend([
+                (cross_in[1, step, part, :], k_half[head], v_half[head], bias_high[...])
+                for head, part in zip(heads, parts)
+            ])
             for head, part, (mixed, top, total) in zip(heads, parts, done):
                 cross_out[2, step, part, :] = jnp.where(
                     by_query, (mixed / total).astype(jnp.bfloat16), v_half[head, LOW, :]
                 )
             stat_out[step] = as_row(
-                jnp.concatenate([top + jnp.log2(total) for mixed, top, total in done[:2]], axis=0)
+                jnp.concatenate([top + jnp.log2(total) for mixed, top, total in done], axis=0)
             )
-            mixed, top, total = done[2]
-            o_half[step] = merge(
-                mixed, top, total, cross_in[0, step].astype(jnp.float32),
-                as_columns(stat_in[step]),
-            ).astype(jnp.bfloat16)
             cross_copy(2, step, peer).start()
             stat_copy(step, peer).start()
+            near = attend([(q_half[step], k_half[step], v_half[step], bias_own[...])])[0]
+            cross_copy(0, step, peer).wait_recv()
+            stat_copy(step, peer).wait_recv()
+            o_half[step] = merge(
+                *near, cross_in[0, step].astype(jnp.float32), as_columns(stat_in[step])
+            ).astype(jnp.bfloat16)
             give((step,))
 
         def high_pair(turn):
             both = (2 * turn, 2 * turn + 1)
+            near = attend([
+                (q_half[steps + step], k_half[steps + step], v_half[steps + step], bias_own[...])
+                for step in both
+            ])
+            low = [scores_of(q_half[steps + step], cross_in[1, step]) for step in both]
+            tops = [jnp.max(scores, axis=1, keepdims=True) for scores in low]
+            low = [weigh(scores, top) for scores, top in zip(low, tops)]
+            totals = [jnp.sum(weights, axis=1, keepdims=True) for weights in low]
             for step in both:
                 cross_copy(2, step, peer).wait_recv()
                 stat_copy(steps + step, peer).wait_recv()
-            done = attend(
-                [
-                    (q_half[steps + step], k_half[steps + step], v_half[steps + step], bias_own[...])
-                    for step in both
-                ]
-                + [
-                    (q_half[steps + step], cross_in[1, step], cross_in[2, step], None)
-                    for step in both
-                ]
-            )
-            for step, near, low in zip(both, done[:2], done[2:]):
+            for step, own, weights, top, total in zip(both, near, low, tops, totals):
                 other = jnp.where(
-                    by_query, cross_in[2, step].astype(jnp.float32), low[0] / low[2]
+                    by_query, cross_in[2, step].astype(jnp.float32),
+                    mix(weights, cross_in[2, step]) / total,
                 )
                 logs = jnp.where(
                     by_query, as_columns(stat_in[steps + step]),
-                    jnp.broadcast_to(low[1] + jnp.log2(low[2]), (pair, HD)),
+                    jnp.broadcast_to(top + jnp.log2(total), (pair, HD)),
                 )
-                o_half[steps + step] = merge(*near, other, logs).astype(jnp.bfloat16)
+                o_half[steps + step] = merge(*own, other, logs).astype(jnp.bfloat16)
             give([steps + step for step in both])
 
         early = steps // 2 + 1
@@ -693,7 +680,7 @@
     dma = pltpu.SemaphoreType.DMA
     return pl.pallas_call(
         cut_kernel,
-        out_shape=jax.ShapeDtypeStruct(queries.shape, jnp.bfloat16),
+        out_shape=pltpu.VMEM(queries.shape, jnp.bfloat16),
         in_specs=[pl.BlockSpec(memory_space=pltpu.SMEM), everything, everything, everything],
         out_specs=pl.BlockSpec(memory_space=pl.ANY),
         scratch_shapes=[pltpu.VMEM((HEADS, pair, HD), jnp.bfloat16)] * 4
@@ -709,7 +696,7 @@
             dma((HEADS,)), dma((HEADS,)), dma((HEADS,)),
         ],
         compiler_params=pltpu.CompilerParams(
-            collective_id=0, has_side_effects=True, vmem_limit_bytes=32 * 1024 * 1024
+            collective_id=0, has_side_effects=True, vmem_limit_bytes=56 * 1024 * 1024
         ),
     )(span_starts, queries, keys, values)
 

time: 60.8 us -> 55.6 us (0.914)
  local copies, waits for them, and re-layouts: 4 us -> 0.82 us
  Pallas kernels: 55.9 us -> 53.9 us
    unnamed x7 -> x1, local copies, waits for them, and re-layouts: 4 us -> 0.82 us
    pallas_call x1, Pallas kernels: 55.9 us -> 53.9 us  [cut_body(): pl.pallas_call(cut_kernel, out_shape=pltpu.VMEM(queries.shape, jnp.bfloat...]
where the time goes in v5:
time: 55.6 us; the launch traced here: 55.4 us
  Pallas kernels  53.9 us (97%)
  local copies, waits for them, and re-layouts  0.82 us (1%)
  between operations  0.66 us (1%)
    pallas_call x1, Pallas kernels, cut_body(): pl.pallas_call(cut_kernel, out_shape=pltpu.VMEM(queries.shape, jnp.bfloat...  53.9 us

profile of v5, /device:TPU:0, one launch (start us, length us, event | category | flops | bytes accessed | tf_op | source)
XLA Modules:
  0.0 55.4 jit_solution(12665056791727636331)
XLA Ops:
  0.7 53.9 %shard_map.46 = bf16[144,2048]{1,0:T(8,128)(2,1)S(1)} custom-call(s32[1]{0:T(128)S(6)} %copy.7.starts_ref, bf16[144,2048]{1,0:T(8,128)(2,1)} %q_ref.1, bf16[144,2048]{1,0:T(8,128)(2,1)} %k_ref.1, bf16[144,2048]{1,0:T(8,128)(2,1)} %v_ref.1), custom_call_target="tpu_custom_call" | custom-call | tf_op jit(solution)/shard_map/pallas_call | solution.py:681
  54.6 0.8 %copy.6 = bf16[144,2048]{1,0:T(8,128)(2,1)} copy(bf16[144,2048]{1,0:T(8,128)(2,1)S(1)} %shard_map.46) | data formatting | bytes 1179648

commit v6 on v5

--- a/solution.py
+++ b/solution.py
@@ -289,7 +289,7 @@
 def cut_kernel(
     starts_ref, q_ref, k_ref, v_ref, out_ref,
     q_half, k_half, v_half, o_half, cross_in, cross_out, stat_in, stat_out,
-    bias_own, bias_low, bias_high,
+    bias_own, bias_low, bias_high, kept,
     half_send, half_recv, half_local, cross_send, cross_recv,
     stat_send, stat_recv, out_send, out_recv, out_local,
 ):
@@ -444,13 +444,18 @@
 
     @pl.when(me == 3)
     def _():
-        repeat(HEADS, lambda head: half_copy(0, head, HIGH, me - 1).start())
+        repeat(steps, lambda head: half_copy(0, head, HIGH, me - 1).start())
 
         def pair_part(head):
             half_copy(1, head, HIGH, me - 1).start()
             half_copy(2, head, HIGH, me - 1).start()
 
-        repeat(HEADS, pair_part)
+        def mixed_part(head):
+            half_copy(0, steps + head, HIGH, me - 1).start()
+            pair_part(head)
+
+        repeat(steps, mixed_part)
+        repeat(steps, lambda head: pair_part(steps + head))
         outer_end(HIGH, me - 1)
 
     def own_start(part):
@@ -590,14 +595,13 @@
                 )
             cross_copy(1, step, peer).start()
 
-        repeat(steps, send_either)
 
         def give(heads):
             for head in heads:
                 result_copy(head, HIGH, outer).start()
                 result_local(head, LOW).start()
 
-        def span_and_low(step):
+        def span_part(step):
             heads = (2 * step, 2 * step + 1)
             parts = (LOW, HIGH)
             cross_copy(1, step, peer).wait_recv()
@@ -617,20 +621,33 @@
             )
             cross_copy(2, step, peer).start()
             stat_copy(step, peer).start()
-            near = attend([(q_half[step], k_half[step], v_half[step], bias_own[...])])[0]
-            cross_copy(0, step, peer).wait_recv()
-            stat_copy(step, peer).wait_recv()
-            o_half[step] = merge(
-                *near, cross_in[0, step].astype(jnp.float32), as_columns(stat_in[step])
-            ).astype(jnp.bfloat16)
-            give((step,))
-
-        def high_pair(turn):
+
+        def low_pair(turn):
+            both = (2 * turn, 2 * turn + 1)
+            near = attend([
+                (q_half[step], k_half[step], v_half[step], bias_own[...]) for step in both
+            ])
+            for step in both:
+                cross_copy(0, step, peer).wait_recv()
+                stat_copy(step, peer).wait_recv()
+            for step, own in zip(both, near):
+                o_half[step] = merge(
+                    *own, cross_in[0, step].astype(jnp.float32), as_columns(stat_in[step])
+                ).astype(jnp.bfloat16)
+            give(both)
+
+        def high_near(turn):
             both = (2 * turn, 2 * turn + 1)
             near = attend([
                 (q_half[steps + step], k_half[steps + step], v_half[steps + step], bias_own[...])
                 for step in both
             ])
+            for step, own in zip(both, near):
+                for kind in range(3):
+                    kept[kind, step] = jnp.broadcast_to(own[kind], (pair, HD))
+
+        def high_pair(turn):
+            both = (2 * turn, 2 * turn + 1)
             low = [scores_of(q_half[steps + step], cross_in[1, step]) for step in both]
             tops = [jnp.max(scores, axis=1, keepdims=True) for scores in low]
             low = [weigh(scores, top) for scores, top in zip(low, tops)]
@@ -638,7 +655,7 @@
             for step in both:
                 cross_copy(2, step, peer).wait_recv()
                 stat_copy(steps + step, peer).wait_recv()
-            for step, own, weights, top, total in zip(both, near, low, tops, totals):
+            for step, weights, top, total in zip(both, low, tops, totals):
                 other = jnp.where(
                     by_query, cross_in[2, step].astype(jnp.float32),
                     mix(weights, cross_in[2, step]) / total,
@@ -647,18 +664,38 @@
                     by_query, as_columns(stat_in[steps + step]),
                     jnp.broadcast_to(top + jnp.log2(total), (pair, HD)),
                 )
-                o_half[steps + step] = merge(*own, other, logs).astype(jnp.bfloat16)
+                o_half[steps + step] = merge(
+                    kept[0, step], kept[1, step], kept[2, step], other, logs
+                ).astype(jnp.bfloat16)
             give([steps + step for step in both])
 
-        early = steps // 2 + 1
-        repeat(early, span_and_low)
+        def send_and_span(step):
+            send_either(2 * step)
+            send_either(2 * step + 1)
+            span_part(step)
+
+        quarter = steps // 2
+        send_and_span(0)
+
+        def early(turn):
+            send_and_span(1 + turn)
+            low_pair(turn)
+
+        repeat(quarter - 1, early)
+        span_part(quarter)
+        low_pair(quarter - 1)
+        high_near(0)
 
         def late(turn):
-            span_and_low(early + turn)
+            span_part(quarter + 1 + turn)
+            high_near(1 + turn)
             high_pair(turn)
 
-        repeat(steps - early, late)
-        high_pair(steps - early)
+        repeat(quarter - 2, late)
+        high_pair(quarter - 2)
+        span_part(steps - 1)
+        high_near(quarter - 1)
+        high_pair(quarter - 1)
 
         def finish(step):
             query_copy(step, peer).wait_send()
@@ -690,6 +727,7 @@
             pltpu.VMEM((pair, pair), jnp.float32),
             pltpu.VMEM((pair, rows), jnp.float32),
             pltpu.VMEM((rows, pair), jnp.float32),
+            pltpu.VMEM((3, steps, pair, HD), jnp.float32),
             dma((3, HEADS)), dma((3, HEADS)), dma((3, HEADS)),
             dma((3, steps)), dma((3, steps)),
             dma((HEADS,)), dma((HEADS,)),

time: 55.6 us -> 57.1 us (1.027)
  Pallas kernels: 53.9 us -> 55.5 us
    pallas_call x1, Pallas kernels: 53.9 us -> 55.5 us  [cut_body(): pl.pallas_call(cut_kernel, out_shape=pltpu.VMEM(queries.shape, jnp.bfloat...]
where the time goes in v6:
time: 57.1 us; the launch traced here: 56.9 us
  Pallas kernels  55.5 us (97%)
  local copies, waits for them, and re-layouts  0.82 us (1%)
  between operations  0.66 us (1%)
    pallas_call x1, Pallas kernels, cut_body(): pl.pallas_call(cut_kernel, out_shape=pltpu.VMEM(queries.shape, jnp.bfloat...  55.5 us

profile of v6, /device:TPU:0, one launch (start us, length us, event | category | flops | bytes accessed | tf_op | source)
XLA Modules:
  0.0 56.9 jit_solution(8874422629779860095)
XLA Ops:
  0.7 55.5 %shard_map.46 = bf16[144,2048]{1,0:T(8,128)(2,1)S(1)} custom-call(s32[1]{0:T(128)S(6)} %copy.7.starts_ref, bf16[144,2048]{1,0:T(8,128)(2,1)} %q_ref.1, bf16[144,2048]{1,0:T(8,128)(2,1)} %k_ref.1, bf16[144,2048]{1,0:T(8,128)(2,1)} %v_ref.1), custom_call_target="tpu_custom_call" | custom-call | tf_op jit(solution)/shard_map/pallas_call | solution.py:718
  56.1 0.8 %copy.6 = bf16[144,2048]{1,0:T(8,128)(2,1)} copy(bf16[144,2048]{1,0:T(8,128)(2,1)S(1)} %shard_map.46) | data formatting | bytes 1179648

commit v7 on v6

--- a/solution.py
+++ b/solution.py
@@ -438,8 +438,13 @@
 
         repeat(steps, lambda step: half_copy(1, steps + step, LOW, me + 1).start())
         repeat(steps, first_part)
-        repeat(steps, lambda step: half_copy(2, steps + step, LOW, me + 1).start())
-        repeat(HEADS, lambda head: half_copy(0, head, LOW, me + 1).start())
+
+        def second_part(step):
+            half_copy(2, steps + step, LOW, me + 1).start()
+            half_copy(0, step, LOW, me + 1).start()
+
+        repeat(steps, second_part)
+        repeat(steps, lambda step: half_copy(0, steps + step, LOW, me + 1).start())
         outer_end(LOW, me + 1)
 
     @pl.when(me == 3)
@@ -526,8 +531,6 @@
             for step in both:
                 cross_copy(2, step, peer).start()
                 stat_copy(steps + step, peer).start()
-
-        repeat(steps // 2, second_part)
 
         def third_part(step):
             heads = (2 * step, 2 * step + 1)
@@ -558,7 +561,12 @@
                 result_copy(head, LOW, outer).start()
                 result_local(head, HIGH).start()
 
-        repeat(steps, third_part)
+        def second_and_third(turn):
+            second_part(turn)
+            third_part(turn)
+
+        repeat(steps // 2, second_and_third)
+        repeat(steps // 2, lambda turn: third_part(steps // 2 + turn))
 
         def finish(step):
             for slot in range(3):

time: 57.1 us -> 56 us (0.981)
  Pallas kernels: 55.5 us -> 54.3 us
    pallas_call x1, Pallas kernels: 55.5 us -> 54.3 us  [cut_body(): pl.pallas_call(cut_kernel, out_shape=pltpu.VMEM(queries.shape, jnp.bfloat...]
where the time goes in v7:
time: 56 us; the launch traced here: 55.8 us
  Pallas kernels  54.3 us (97%)
  local copies, waits for them, and re-layouts  0.82 us (1%)
  between operations  0.66 us (1%)
    pallas_call x1, Pallas kernels, cut_body(): pl.pallas_call(cut_kernel, out_shape=pltpu.VMEM(queries.shape, jnp.bfloat...  54.3 us

profile of v7, /device:TPU:0, one launch (start us, length us, event | category | flops | bytes accessed | tf_op | source)
XLA Modules:
  0.0 55.8 jit_solution(8018627438980312900)
XLA Ops:
  0.7 54.3 %shard_map.46 = bf16[144,2048]{1,0:T(8,128)(2,1)S(1)} custom-call(s32[1]{0:T(128)S(6)} %copy.7.starts_ref, bf16[144,2048]{1,0:T(8,128)(2,1)} %q_ref.1, bf16[144,2048]{1,0:T(8,128)(2,1)} %k_ref.1, bf16[144,2048]{1,0:T(8,128)(2,1)} %v_ref.1), custom_call_target="tpu_custom_call" | custom-call | tf_op jit(solution)/shard_map/pallas_call | solution.py:726
  55.0 0.8 %copy.6 = bf16[144,2048]{1,0:T(8,128)(2,1)} copy(bf16[144,2048]{1,0:T(8,128)(2,1)S(1)} %shard_map.46) | data formatting | bytes 1179648

commit v8 on v7

--- a/solution.py
+++ b/solution.py
@@ -514,40 +514,31 @@
 
         repeat(steps // 2, first_part)
 
-        def second_part(turn):
-            both = (2 * turn, 2 * turn + 1)
-            for step in both:
-                arrived(2, steps + step)
-                cross_copy(1, step, peer).wait_recv()
-            done = attend([
-                (cross_in[1, step], k_half[steps + step], v_half[steps + step], None)
-                for step in both
-            ])
-            for step, (mixed, top, total) in zip(both, done):
-                cross_out[2, step] = jnp.where(
-                    by_query, (mixed / total).astype(jnp.bfloat16), v_half[steps + step]
-                )
-                stat_out[steps + step] = as_row(top + jnp.log2(total))
-            for step in both:
-                cross_copy(2, step, peer).start()
-                stat_copy(steps + step, peer).start()
-
-        def third_part(step):
-            heads = (2 * step, 2 * step + 1)
-            parts = (LOW, HIGH)
-            for head in heads:
+        def near_items(step):
+            return [
+                (q_half[head], k_half[head], v_half[head], bias_own[...])
+                for head in (2 * step, 2 * step + 1)
+            ]
+
+        def far_items(step):
+            return [
+                (q_half[2 * step + side], cross_in[1, step, part, :],
+                 cross_in[2, step, part, :], bias_low[...])
+                for side, part in enumerate((LOW, HIGH))
+            ]
+
+        def near_arrived(step):
+            for head in (2 * step, 2 * step + 1):
                 arrived(0, head)
-            near = attend([
-                (q_half[head], k_half[head], v_half[head], bias_own[...]) for head in heads
-            ])
+
+        def far_arrived(step):
             cross_copy(2, step, peer).wait_recv()
             stat_copy(step, peer).wait_recv()
+
+        def settle(step, near, far):
             logs = as_columns(jnp.where(by_query, stat_in[step], -1e30))
-            far = attend([
-                (q_half[head], cross_in[1, step, part, :], cross_in[2, step, part, :], bias_low[...])
-                for head, part in zip(heads, parts)
-            ])
-            for head, part, own, span in zip(heads, parts, near, far):
+            heads = (2 * step, 2 * step + 1)
+            for head, part, own, span in zip(heads, (LOW, HIGH), near, far):
                 top = jnp.maximum(own[1], span[1])
                 mine, theirs = jnp.exp2(own[1] - top), jnp.exp2(span[1] - top)
                 mixed = own[0] * mine + span[0] * theirs
@@ -561,12 +552,37 @@
                 result_copy(head, LOW, outer).start()
                 result_local(head, HIGH).start()
 
-        def second_and_third(turn):
-            second_part(turn)
-            third_part(turn)
-
-        repeat(steps // 2, second_and_third)
-        repeat(steps // 2, lambda turn: third_part(steps // 2 + turn))
+        def second_part(turn):
+            both = (2 * turn, 2 * turn + 1)
+            for step in both:
+                arrived(2, steps + step)
+                cross_copy(1, step, peer).wait_recv()
+            near_arrived(turn)
+            done = attend([
+                (cross_in[1, step], k_half[steps + step], v_half[steps + step], None)
+                for step in both
+            ] + near_items(turn))
+            for step, (mixed, top, total) in zip(both, done):
+                cross_out[2, step] = jnp.where(
+                    by_query, (mixed / total).astype(jnp.bfloat16), v_half[steps + step]
+                )
+                stat_out[steps + step] = as_row(top + jnp.log2(total))
+            for step in both:
+                cross_copy(2, step, peer).start()
+                stat_copy(steps + step, peer).start()
+            far_arrived(turn)
+            settle(turn, done[2:], attend(far_items(turn)))
+
+        repeat(steps // 2, second_part)
+        near_arrived(steps // 2)
+        near = attend(near_items(steps // 2))
+        for step in range(steps // 2, steps):
+            if step + 1 < steps:
+                near_arrived(step + 1)
+            far_arrived(step)
+            done = attend(far_items(step) + (near_items(step + 1) if step + 1 < steps else []))
+            settle(step, near, done[:2])
+            near = done[2:]
 
         def finish(step):
             for slot in range(3):

time: 56 us -> 56 us (level)
  no operation moved by 1% of the time
where the time goes in v8:
time: 56 us; the launch traced here: 55.8 us
  Pallas kernels  54.3 us (97%)
  local copies, waits for them, and re-layouts  0.82 us (1%)
  between operations  0.66 us (1%)
    pallas_call x1, Pallas kernels, cut_body(): pl.pallas_call(cut_kernel, out_shape=pltpu.VMEM(queries.shape, jnp.bfloat...  54.3 us

profile of v8, /device:TPU:0, one launch (start us, length us, event | category | flops | bytes accessed | tf_op | source)
XLA Modules:
  0.0 55.8 jit_solution(17228362059155190962)
XLA Ops:
  0.7 54.3 %shard_map.46 = bf16[144,2048]{1,0:T(8,128)(2,1)S(1)} custom-call(s32[1]{0:T(128)S(6)} %copy.7.starts_ref, bf16[144,2048]{1,0:T(8,128)(2,1)} %q_ref.1, bf16[144,2048]{1,0:T(8,128)(2,1)} %k_ref.1, bf16[144,2048]{1,0:T(8,128)(2,1)} %v_ref.1), custom_call_target="tpu_custom_call" | custom-call | tf_op jit(solution)/shard_map/pallas_call | solution.py:742
  54.9 0.8 %copy.6 = bf16[144,2048]{1,0:T(8,128)(2,1)} copy(bf16[144,2048]{1,0:T(8,128)(2,1)S(1)} %shard_map.46) | data formatting | bytes 1179648

commit v9 on v8

--- a/solution.py
+++ b/solution.py
@@ -716,8 +716,8 @@
             high_pair(turn)
 
         repeat(quarter - 2, late)
+        span_part(steps - 1)
         high_pair(quarter - 2)
-        span_part(steps - 1)
         high_near(quarter - 1)
         high_pair(quarter - 1)
 

time: 56 us -> 55.1 us (0.984)
  Pallas kernels: 54.3 us -> 53.5 us
    pallas_call x1, Pallas kernels: 54.3 us -> 53.5 us  [cut_body(): pl.pallas_call(cut_kernel, out_shape=pltpu.VMEM(queries.shape, jnp.bfloat...]
where the time goes in v9:
time: 55.1 us; the launch traced here: 54.9 us
  Pallas kernels  53.5 us (97%)
  local copies, waits for them, and re-layouts  0.82 us (1%)
  between operations  0.66 us (1%)
    pallas_call x1, Pallas kernels, cut_body(): pl.pallas_call(cut_kernel, out_shape=pltpu.VMEM(queries.shape, jnp.bfloat...  53.5 us

profile of v9, /device:TPU:0, one launch (start us, length us, event | category | flops | bytes accessed | tf_op | source)
XLA Modules:
  0.0 54.9 jit_solution(5777175221148941882)
XLA Ops:
  0.7 53.5 %shard_map.46 = bf16[144,2048]{1,0:T(8,128)(2,1)S(1)} custom-call(s32[1]{0:T(128)S(6)} %copy.7.starts_ref, bf16[144,2048]{1,0:T(8,128)(2,1)} %q_ref.1, bf16[144,2048]{1,0:T(8,128)(2,1)} %k_ref.1, bf16[144,2048]{1,0:T(8,128)(2,1)} %v_ref.1), custom_call_target="tpu_custom_call" | custom-call | tf_op jit(solution)/shard_map/pallas_call | solution.py:742
  54.1 0.8 %copy.6 = bf16[144,2048]{1,0:T(8,128)(2,1)} copy(bf16[144,2048]{1,0:T(8,128)(2,1)S(1)} %shard_map.46) | data formatting | bytes 1179648
